TPU v7x, 256 devices: a whole 4x4x8 slice. The times are simulated.
256 devices in a mesh: ctx: 32 (over x, z), tp: 8 (over y, core).
Axes of the slice: x: 4, y: 4, z: 8, core: 2. Of those that a mesh axis runs over, the one named last changes fastest.
Arguments:
- queries: bfloat16 [4096, 8192], P('ctx', 'tp'), may hold values from -160 to 160
- key_rows: bfloat16 [4096, 1024], P('ctx', 'tp'), may hold values from -4.5 to 4.5
- value_rows: bfloat16 [4096, 1024], P('ctx', 'tp'), may hold values from -6 to 6
- doc_lengths: int32 [16], replicated, may hold values from 1 to 2112, 4096 in all
- gate_input: bfloat16 [4096, 8192], P('ctx', 'tp'), may hold values from -6 to 6
- bc_input: bfloat16 [4096, 2, 4, 256], P('ctx'), may hold values from -1.796875 to 1.796875
- step_size: float32 [4096, 128], P('ctx', 'tp'), may hold values from 0.5 to 2
- decay_rate: float32 [128], P('tp'), may hold values from 0 to 1, as said below
- skip_gain: float32 [128], P('tp'), may hold values from 1 to 4
- conv_x: float32 [4, 8192], P(None, 'tp'), may hold values from -3 to 3
- conv_bc: float32 [4, 2, 4, 256], replicated, may hold values from -3 to 3
- norm_gain: float32 [8192], P('tp'), may hold values from 0.1 to 1.9
Outputs:
- mixed: bfloat16 [4096, 8192], P('ctx', 'tp')
Inputs may be any that keep to these rules, and one draw needn't show every extreme that they name: `doc_lengths`: documents lie end to end in token order; the longest has exactly 2112 tokens. `decay_rate`: positive rates.
All inputs are finite; a program needn't handle non-finite values.
Results may differ from a plain program's by a relative error of at most 0.02.
Values may be sent and summed in bfloat16 or wider, within the bound.
No kernel may reach another device: no remote copies, remote signals or barrier semaphores. Data moves between devices by JAX's collectives and lax.ppermute only.
A program may use at most 128 MiB of HBM per device.

v0:
```python
import math

import jax
import jax.numpy as jnp
from jax import lax
from jax.experimental import pallas as pl
from jax.experimental.pallas import tpu as pltpu
from jax.sharding import PartitionSpec as P

EPSILON = 1e-05
NEGATIVE_FILL = -1e30
NEAR = 8
FAR = 4
SHARD = 128
ROW = NEAR * SHARD
CHUNK = 256
CHUNKS = ROW // CHUNK
HEAD = 128
STATE = 256
RIM = 16
PAST = 10 * CHUNK
WIDE = 256
STEPS_AT = SHARD + RIM
BC_AT = STEPS_AT + 16
PACK_ROWS = BC_AT + 2 * SHARD
EXP2_SCALE = math.log2(math.e) / math.sqrt(HEAD)
F32 = jnp.float32
BF16 = jnp.bfloat16


def near_groups():
    return [[x * NEAR + z for z in range(NEAR)] for x in range(FAR)]


def far_groups():
    return [[x * NEAR + z for x in range(FAR)] for z in range(NEAR)]


def exchange_near(x):
    return lax.all_to_all(x, "ctx", 0, 0, axis_index_groups=near_groups(), tiled=True)


def from_row_behind(x, by):
    pairs = [(x0 * NEAR + z, (x0 + by) * NEAR + z) for x0 in range(FAR - by) for z in range(NEAR)]
    return lax.ppermute(x, "ctx", pairs)


def from_shard_behind(x):
    return lax.ppermute(x, "ctx", [(i, i + 1) for i in range(NEAR * FAR - 1)])


def with_partner(x):
    count = lax.axis_size("tp")
    return lax.ppermute(x, "tp", [(t, t ^ 1) for t in range(count)])


def first_tokens(docs, pos):
    begin = jnp.int32(0)
    first = pos
    for d in range(docs.shape[0]):
        first = jnp.where(pos >= begin, begin, first)
        begin = begin + docs[d]
    return first


def columns_of(rows):
    count = rows[0].shape[1]
    rows = list(rows) + [jnp.zeros((1, count), F32)] * (8 - len(rows))
    return jnp.transpose(jnp.concatenate(rows, 0))


def silu(v):
    return v / (1.0 + jnp.exp(-v))


def pair_kernel(keys, values, out, sems):
    copies = []
    for n in range(NEAR):
        copies.append(pltpu.make_async_copy(keys, out.at[n, :, pl.ds(0, HEAD)], sems.at[2 * n]))
        copies.append(
            pltpu.make_async_copy(values, out.at[n, :, pl.ds(HEAD, HEAD)], sems.at[2 * n + 1])
        )
    for copy in copies:
        copy.start()
    for copy in copies:
        copy.wait()


def pack_kernel(info, docs, queries, steps, raw, rim, taps, out, ext):
    ext[0:RIM] = rim[:, NEAR * HEAD :].astype(F32)
    ext[RIM:] = raw[...].astype(F32)
    pos = info[3] + lax.broadcasted_iota(jnp.int32, (1, SHARD), 1)
    since = columns_of([(pos - first_tokens(docs, pos)).astype(F32)])[:, 0:1]
    acc = jnp.zeros((SHARD, STATE), F32)
    for m in range(4):
        part = ext[RIM - m : RIM - m + SHARD] * taps[3 - m : 4 - m]
        acc = acc + jnp.where(since >= m, part, 0.0)
    convolved = silu(acc).astype(BF16)
    wide = jnp.concatenate([steps[...], jnp.zeros((SHARD, HEAD - 2 * NEAR), F32)], 1)
    rows = jnp.transpose(wide)
    high = rows.astype(BF16).astype(F32)
    middle = (rows - high).astype(BF16).astype(F32)
    low = rows - high - middle
    for n in range(NEAR):
        out[n, 0:SHARD] = queries[:, n * HEAD : (n + 1) * HEAD]
        two = slice(2 * n, 2 * n + 2)
        out[n, SHARD:STEPS_AT] = rim[:, n * HEAD : (n + 1) * HEAD]
        out[n, STEPS_AT:BC_AT] = jnp.concatenate(
            [high[two], middle[two], low[two], jnp.zeros((10, HEAD), F32)], 0
        ).astype(BF16)
        out[n, BC_AT : BC_AT + SHARD] = convolved[:, 0:HEAD]
        out[n, BC_AT + SHARD :] = convolved[:, HEAD:]


def two_heads(first, second, shape):
    lane = lax.broadcasted_iota(jnp.int32, shape, 1)
    return jnp.where(lane < HEAD // 2, jnp.broadcast_to(first, shape), jnp.broadcast_to(second, shape))


def steps_of(received):
    pieces = []
    for s in range(NEAR):
        piece = received[s, STEPS_AT:BC_AT].astype(F32)
        pieces.append(piece[0:2] + piece[2:4] + piece[4:6])
    return jnp.concatenate(pieces, 1)


def decays_of(steps, rates, near):
    rate = jnp.concatenate(
        [jnp.full((1, ROW), rates[2 * near], F32), jnp.full((1, ROW), rates[2 * near + 1], F32)], 0
    )
    log_decay = jnp.concatenate([-rate * steps, jnp.zeros((6, ROW), F32)], 0)
    below = lax.broadcasted_iota(jnp.int32, (CHUNK, CHUNK), 0)
    across = lax.broadcasted_iota(jnp.int32, (CHUNK, CHUNK), 1)
    upper = jnp.where(below <= across, 1.0, 0.0).astype(F32)
    locals_ = [
        jnp.dot(
            log_decay[:, k * CHUNK : (k + 1) * CHUNK],
            upper,
            precision=lax.Precision.HIGHEST,
            preferred_element_type=F32,
        )[0:2]
        for k in range(CHUNKS)
    ]
    return locals_, [local[:, CHUNK - 1 : CHUNK] for local in locals_]


def weights_kernel(info, docs, rates, received, weigh, decays, since, seen):
    steps = steps_of(received)
    locals_, totals = decays_of(steps, rates, info[1])
    row_start = info[0]
    pos = row_start + lax.broadcasted_iota(jnp.int32, (1, ROW), 1)
    first = first_tokens(docs, pos)
    decay_rows = []
    for k in range(CHUNKS):
        rows = slice(k * CHUNK, (k + 1) * CHUNK)
        last_start = first[:, (k + 1) * CHUNK - 1 : (k + 1) * CHUNK]
        gap = jnp.where(pos[:, rows] >= last_start, totals[k] - locals_[k], NEGATIVE_FILL)
        w = jnp.exp(gap) * steps[:, rows]
        begin = first[:, rows]
        columns = columns_of(
            [w[0:1], w[1:2], (pos[:, rows] - begin).astype(F32), (begin - row_start).astype(F32)]
        )
        weigh[rows] = two_heads(columns[:, 0:1], columns[:, 1:2], (CHUNK, HEAD))
        since[rows] = jnp.broadcast_to(columns[:, 2:3], (CHUNK, HEAD))
        seen[rows] = jnp.broadcast_to(columns[:, 3:4], (CHUNK, HEAD))
        crossing = jnp.where(last_start < row_start + k * CHUNK, jnp.exp(totals[k]), 0.0)
        decay_rows.append(jnp.broadcast_to(crossing, (2, STATE)))
    whole = totals[0] + totals[1] + totals[2] + totals[3]
    last = jnp.where(first[:, ROW - 1 : ROW] < row_start, jnp.exp(whole), 0.0)
    decay_rows.append(jnp.broadcast_to(last, (2, STATE)))
    decays[...] = jnp.concatenate(decay_rows + [jnp.zeros((6, STATE), F32)], 0)


def two_head_rows(pair):
    shape = (HEAD, STATE)
    channel = lax.broadcasted_iota(jnp.int32, shape, 0)
    return jnp.where(
        channel < HEAD // 2,
        jnp.broadcast_to(pair[0:1], shape),
        jnp.broadcast_to(pair[1:2], shape),
    )


def dot_rows(left, right):
    return lax.dot_general(left, right, (((1,), (1,)), ((), ())), preferred_element_type=F32)


def chunk_of(choose_mine, received, other, k):
    halves = []
    two = slice(2 * k, 2 * k + 2)
    for half in range(2):
        mine = received[two, BC_AT + half * SHARD : BC_AT + (half + 1) * SHARD]
        theirs = other[two, half * SHARD : (half + 1) * SHARD]
        halves.append(jnp.where(choose_mine, mine, theirs))
    return jnp.concatenate([half.reshape(CHUNK, HEAD) for half in halves], 1)


def attend_kernel(
    info,
    docs,
    received,
    own,
    back1,
    back2a,
    back2b,
    back3,
    seen,
    attended,
    top,
    total,
    summed,
    halo_seen,
    halo_top,
    halo_total,
    halo_summed,
):
    row_start = info[0]
    halo_pos = row_start - RIM + lax.broadcasted_iota(jnp.int32, (1, HEAD), 1)
    halo_first = columns_of([(first_tokens(docs, halo_pos) - row_start).astype(F32)])
    halo_seen[...] = jnp.broadcast_to(halo_first[0:RIM, 0:1], (RIM, HEAD))
    begin = jnp.int32(0)
    cross_start, cross_end = jnp.int32(0), jnp.int32(0)
    for d in range(docs.shape[0]):
        inside = begin <= row_start
        cross_start = jnp.where(inside, begin, cross_start)
        begin = begin + docs[d]
        cross_end = jnp.where(inside, begin, cross_end)
    reached = cross_end - row_start
    wide_blocks = PAST // WIDE
    lowest = lax.div(cross_start - row_start + PAST, jnp.int32(WIDE))

    def masked(raw, offset, seen_rows, diagonal):
        count = raw.shape[0]
        slabs = []
        for n in range(raw.shape[1] // HEAD):
            place = lax.broadcasted_iota(jnp.int32, (1, HEAD), 1) + (offset + n * HEAD)
            visible = place.astype(F32) >= seen_rows
            if diagonal is not None:
                down = lax.broadcasted_iota(jnp.int32, (count, HEAD), 0) + diagonal
                along = lax.broadcasted_iota(jnp.int32, (count, HEAD), 1) + n * HEAD
                visible = visible & (along <= down)
            slabs.append(jnp.where(visible, raw[:, n * HEAD : (n + 1) * HEAD], NEGATIVE_FILL))
        return slabs

    def largest_of(slabs):
        most = slabs[0]
        for slab in slabs[1:]:
            most = jnp.maximum(most, slab)
        return jnp.max(most, axis=1, keepdims=True)

    def weighed(slabs, new_top):
        parts, sums = [], None
        for slab in slabs:
            weight = jnp.exp2((slab - new_top) * EXP2_SCALE)
            sums = weight if sums is None else sums + weight
            parts.append(weight.astype(BF16))
        return sums, parts

    def fold(query, keys, block, within, seen_ref, top_ref, total_ref, summed_ref, rows, diagonal):
        at = pl.ds(pl.multiple_of(within * WIDE, WIDE), WIDE)
        raw = dot_rows(query, keys[at, 0:HEAD])
        slabs = masked(raw, block * WIDE - PAST, seen_ref[rows], diagonal)
        old_top = top_ref[rows]
        new_top = jnp.maximum(old_top, largest_of(slabs))
        factor = jnp.exp2((old_top - new_top) * EXP2_SCALE)
        sums, parts = weighed(slabs, new_top)
        product = jnp.dot(
            jnp.concatenate(parts, 1), keys[at, HEAD:], preferred_element_type=F32
        )
        top_ref[rows] = new_top
        total_ref[rows] = total_ref[rows] * factor + sums
        summed_ref[rows] = summed_ref[rows] * factor + product

    raws, weights = [], [[] for _ in range(CHUNKS)]
    for j in range(CHUNKS):
        query = received[2 * j :, 0:SHARD, :].reshape(ROW - j * CHUNK, HEAD)
        at = slice(j * CHUNK, (j + 1) * CHUNK)
        raws.append(dot_rows(query, own[at, 0:HEAD]))
    for i in range(CHUNKS):
        rows = slice(i * CHUNK, (i + 1) * CHUNK)
        slabs = []
        for j in range(i + 1):
            raw = raws[j][(i - j) * CHUNK : (i - j + 1) * CHUNK]
            slabs += masked(raw, j * CHUNK, seen[rows], 0 if i == j else None)
        first_top = jnp.broadcast_to(largest_of(slabs), (CHUNK, HEAD))
        sums, parts = weighed(slabs, first_top)
        top[rows] = first_top
        total[rows] = sums
        for j in range(i + 1):
            weights[j].append(jnp.concatenate(parts[2 * j : 2 * j + 2], 1))
    for j in range(CHUNKS):
        values = own[j * CHUNK : (j + 1) * CHUNK, HEAD:]
        product = jnp.dot(jnp.concatenate(weights[j], 0), values, preferred_element_type=F32)
        rows = slice(j * CHUNK, ROW)
        summed[rows] = product if j == 0 else summed[rows] + product
    halo_top[...] = jnp.full((RIM, HEAD), NEGATIVE_FILL, F32)
    halo_total[...] = jnp.zeros((RIM, HEAD), F32)
    halo_summed[...] = jnp.zeros((RIM, HEAD), F32)

    def earlier(count):
        query = received[0 : 2 * count, 0:SHARD, :].reshape(count * CHUNK, HEAD)
        for keys, begin in ((back1, 6), (back2b, 4), (back2a, 2), (back3, 0)):
            blocks = keys.shape[0] // WIDE

            def visit(n, carry):
                within = blocks - 1 - n
                block = begin + within
                fold(
                    query, keys, block, within, seen, top, total, summed, slice(0, count * CHUNK), None
                )
                fold(
                    received[0, SHARD:STEPS_AT],
                    keys,
                    block,
                    within,
                    halo_seen,
                    halo_top,
                    halo_total,
                    halo_summed,
                    slice(0, RIM),
                    (PAST - RIM) - block * WIDE,
                )
                return carry

            lax.fori_loop(0, jnp.clip(begin + blocks - lowest, 0, blocks), visit, 0)

    @pl.when(reached <= CHUNK)
    def _():
        earlier(1)

    @pl.when((reached > CHUNK) & (reached <= 2 * CHUNK))
    def _():
        earlier(2)

    @pl.when(reached > 2 * CHUNK)
    def _():
        earlier(CHUNKS)

    def finish(total_ref, summed_ref):
        whole = jnp.sum(total_ref[...], axis=1, keepdims=True)
        return (summed_ref[...] / jnp.maximum(whole, 0.5)).astype(BF16)

    attended[0:RIM] = finish(halo_total, halo_summed)
    attended[RIM:] = finish(total, summed)


def scan_kernel(
    info, attended, received, other, taps, weigh, decays, since, x_out, states, handed, ext
):
    ext[...] = attended[...].astype(F32)
    near = info[1]
    own_taps = taps[:, pl.ds(pl.multiple_of(near * HEAD, HEAD), HEAD)]
    core_zero = info[2] == 0
    state = jnp.zeros((HEAD, STATE), F32)
    for k in range(CHUNKS):
        rows = slice(k * CHUNK, (k + 1) * CHUNK)
        acc = jnp.zeros((CHUNK, HEAD), F32)
        for m in range(4):
            part = ext[RIM - m + k * CHUNK : RIM - m + (k + 1) * CHUNK] * own_taps[3 - m : 4 - m]
            acc = acc + jnp.where(since[rows] >= m, part, 0.0)
        x = silu(acc).astype(BF16)
        x_out[rows] = x
        states[k] = state.astype(BF16)
        weighed = (x.astype(F32) * weigh[rows]).astype(BF16)
        added = lax.dot_general(
            weighed,
            chunk_of(core_zero, received, other, k),
            (((0,), (0,)), ((), ())),
            preferred_element_type=F32,
        )
        state = state * two_head_rows(decays[2 * k : 2 * k + 2]) + added
    decay = decays[2 * CHUNKS : 2 * CHUNKS + 2]
    high = decay.astype(BF16).astype(F32)
    tail = jnp.concatenate([high, decay - high, jnp.zeros((12, STATE), F32)], 0).astype(BF16)
    state = state.astype(BF16)
    for r in range(FAR):
        handed[r, 0:HEAD] = state
        handed[r, HEAD:] = tail


def inner_kernel(
    info, docs, rates, skip, received, other, x_in, states, y_out, enter_row, c_out
):
    near = info[1]
    core_zero = info[2] == 0
    steps = steps_of(received)
    locals_, totals = decays_of(steps, rates, near)
    row_start = info[0]
    pos = row_start + lax.broadcasted_iota(jnp.int32, (1, ROW), 1)
    first = first_tokens(docs, pos)
    below = lax.broadcasted_iota(jnp.int32, (CHUNK, CHUNK), 0)
    across = lax.broadcasted_iota(jnp.int32, (CHUNK, CHUNK), 1)
    causal = across <= below
    place = across.astype(F32)
    gain = two_heads(skip[2 * near], skip[2 * near + 1], (1, HEAD))
    shape = (CHUNK, HEAD)
    before = jnp.zeros((2, 1), F32)
    for k in range(CHUNKS):
        rows = slice(k * CHUNK, (k + 1) * CHUNK)
        chunk_start = row_start + k * CHUNK
        local = locals_[k]
        e_chunk = jnp.exp(jnp.where(first[:, rows] < chunk_start, local, NEGATIVE_FILL))
        e_row = jnp.exp(jnp.where(first[:, rows] < row_start, before + local, NEGATIVE_FILL))
        before = before + totals[k]
        columns = jnp.transpose(jnp.concatenate([e_chunk, e_row, local, jnp.zeros((2, CHUNK), F32)], 0))
        since = columns_of([(first[:, rows] - chunk_start).astype(F32)])[:, 0:1]
        enter_row[rows] = two_heads(columns[:, 2:3], columns[:, 3:4], shape)
        c_values = chunk_of(jnp.logical_not(core_zero), received, other, k)
        c_out[rows] = c_values
        gram = dot_rows(c_values, chunk_of(core_zero, received, other, k))
        visible = causal & (place >= since)
        x = x_in[rows]
        halves = []
        for h in range(2):
            gap = jnp.where(visible, columns[:, 4 + h : 5 + h] - local[h : h + 1], NEGATIVE_FILL)
            mix = (gram * jnp.exp(gap) * steps[h : h + 1, rows]).astype(BF16)
            halves.append(jnp.dot(mix, x, preferred_element_type=F32))
        lane = lax.broadcasted_iota(jnp.int32, shape, 1)
        y = jnp.where(lane < HEAD // 2, halves[0], halves[1]) + x.astype(F32) * gain
        if k > 0:
            carried = dot_rows(c_values, states[k])
            y = y + two_heads(columns[:, 0:1], columns[:, 1:2], shape) * carried
        y_out[rows] = y


def carried_kernel(info, y_in, enter_row, c_in, handed, y_out):
    entering = jnp.zeros((HEAD, STATE), F32)
    for r in range(FAR - 1):
        tail = handed[r, HEAD:].astype(F32)
        decay = two_head_rows(tail[0:2] + tail[2:4])
        following = entering * decay + handed[r, 0:HEAD].astype(F32)
        entering = jnp.where(r * ROW < info[0], following, entering)
    entering = entering.astype(BF16)
    for k in range(CHUNKS):
        rows = slice(k * CHUNK, (k + 1) * CHUNK)
        carried = dot_rows(c_in[rows], entering)
        y_out[rows] = (y_in[rows] + enter_row[rows] * carried).astype(BF16)


def gated_of(y, gate, h):
    return y[h].astype(F32) * silu(gate[:, h * HEAD : (h + 1) * HEAD].astype(F32))


def square_kernel(y, gate, sums):
    acc = jnp.zeros((SHARD, HEAD), F32)
    for h in range(NEAR):
        gated = gated_of(y, gate, h)
        acc = acc + gated * gated
    sums[...] = jnp.broadcast_to(jnp.sum(acc, axis=1, keepdims=True), (SHARD, HEAD))


def norm_kernel(y, gate, sums, partner, gain, out):
    mean = (sums[...] + partner[...]) / (2.0 * NEAR * HEAD)
    scale = lax.rsqrt(mean + EPSILON)
    for h in range(NEAR):
        columns = slice(h * HEAD, (h + 1) * HEAD)
        out[:, columns] = (gated_of(y, gate, h) * scale * gain[:, columns]).astype(BF16)


def call(kernel, outs, args, smem=0, raw=(), raw_out=False, scratch=(), flops=0, mib=16):
    specs = []
    for n in range(len(args)):
        if n < smem:
            specs.append(pl.BlockSpec(memory_space=pltpu.SMEM))
        elif n in raw:
            specs.append(pl.BlockSpec(memory_space=pl.ANY))
        else:
            specs.append(pl.BlockSpec(memory_space=pltpu.VMEM))
    single = len(outs) == 1
    shapes = [jax.ShapeDtypeStruct(shape, kind) for shape, kind in outs]
    out_specs = [pl.BlockSpec(memory_space=pl.ANY if raw_out else pltpu.VMEM)] * len(outs)
    return pl.pallas_call(
        kernel,
        out_shape=shapes[0] if single else shapes,
        in_specs=specs,
        out_specs=out_specs[0] if single else out_specs,
        scratch_shapes=list(scratch),
        compiler_params=pltpu.CompilerParams(vmem_limit_bytes=mib * 1024 * 1024),
        cost_estimate=pl.CostEstimate(flops=flops, bytes_accessed=1 << 21, transcendentals=0),
    )(*args)


def run_attend(info, docs, received, own, back1, back2a, back2b, back3, seen):
    return call(
        attend_kernel,
        [((RIM + ROW, HEAD), BF16)],
        (info, docs, received, own, back1, back2a, back2b, back3, seen),
        smem=2,
        scratch=[
            pltpu.VMEM((ROW, HEAD), F32),
            pltpu.VMEM((ROW, HEAD), F32),
            pltpu.VMEM((ROW, HEAD), F32),
            pltpu.VMEM((RIM, HEAD), F32),
            pltpu.VMEM((RIM, HEAD), F32),
            pltpu.VMEM((RIM, HEAD), F32),
            pltpu.VMEM((RIM, HEAD), F32),
        ],
        flops=1 << 32,
        mib=24,
    )


def run_scan(info, attended, received, other, taps, weigh, decays, since):
    return call(
        scan_kernel,
        [
            ((ROW, HEAD), BF16),
            ((CHUNKS, HEAD, STATE), BF16),
            ((FAR, HEAD + 16, STATE), BF16),
        ],
        (info, attended, received, other, taps, weigh, decays, since),
        smem=1,
        scratch=[pltpu.VMEM((RIM + ROW, HEAD), F32)],
    )


def on_device(
    queries,
    key_rows,
    value_rows,
    doc_lengths,
    gate_input,
    bc_input,
    step_size,
    decay_rate,
    skip_gain,
    conv_x,
    conv_bc,
    norm_gain,
):
    ctx = lax.axis_index("ctx")
    tp = lax.axis_index("tp")
    near = ctx % NEAR
    core = tp % 2
    group = tp // 2
    info = jnp.stack([(ctx // NEAR) * ROW, near, core, ctx * SHARD]).astype(jnp.int32)

    bc_mine = lax.dynamic_slice(bc_input, (0, core, group, 0), (SHARD, 1, 1, STATE)).reshape(
        SHARD, STATE
    )
    taps_mine = lax.dynamic_slice(conv_bc, (0, core, group, 0), (4, 1, 1, STATE)).reshape(4, STATE)
    rim = from_shard_behind(jnp.concatenate([queries[SHARD - RIM :], bc_mine[SHARD - RIM :]], 1))
    own = exchange_near(
        call(
            pair_kernel,
            [((NEAR, SHARD, 2 * HEAD), BF16)],
            (key_rows, value_rows),
            raw=(0, 1),
            raw_out=True,
            scratch=[pltpu.SemaphoreType.DMA((2 * NEAR,))],
        ).reshape(ROW, 2 * HEAD)
    )
    packed = call(
        pack_kernel,
        [((NEAR, PACK_ROWS, HEAD), BF16)],
        (info, doc_lengths, queries, step_size, bc_mine, rim, taps_mine),
        smem=2,
        scratch=[pltpu.VMEM((RIM + SHARD, STATE), F32)],
    )
    own, packed = lax.optimization_barrier((own, packed))
    half = ROW // 2
    back1 = from_row_behind(own, 1)
    back2a = from_row_behind(own[:half], 2)
    back2b = from_row_behind(own[half:], 2)
    back3 = from_row_behind(own[half:], 3)
    received = exchange_near(packed.reshape(NEAR * PACK_ROWS, HEAD)).reshape(
        NEAR, PACK_ROWS, HEAD
    )
    weigh, decays, since, seen = call(
        weights_kernel,
        [((ROW, HEAD), F32), ((16, STATE), F32), ((ROW, HEAD), F32), ((ROW, HEAD), F32)],
        (info, doc_lengths, decay_rate, received),
        smem=3,
    )
    received, weigh, back1, back2a, back2b, back3 = lax.optimization_barrier(
        (received, weigh, back1, back2a, back2b, back3)
    )
    other = with_partner(received[:, BC_AT:])
    attended = run_attend(info, doc_lengths, received, own, back1, back2a, back2b, back3, seen)
    x, states, handed = run_scan(info, attended, received, other, conv_x, weigh, decays, since)
    handed = lax.all_to_all(
        handed.reshape(FAR * (HEAD + 16), STATE),
        "ctx",
        0,
        0,
        axis_index_groups=far_groups(),
        tiled=True,
    ).reshape(FAR, HEAD + 16, STATE)
    y_inner, enter_row, c_row = call(
        inner_kernel,
        [((ROW, HEAD), F32), ((ROW, HEAD), F32), ((ROW, STATE), BF16)],
        (info, doc_lengths, decay_rate, skip_gain, received, other, x, states),
        smem=4,
        flops=1 << 30,
    )
    y_row = call(
        carried_kernel,
        [((ROW, HEAD), BF16)],
        (info, y_inner, enter_row, c_row, handed),
        smem=1,
    )
    y_heads = exchange_near(y_row).reshape(NEAR, SHARD, HEAD)
    sums = call(square_kernel, [((SHARD, HEAD), F32)], (y_heads, gate_input))
    partner = with_partner(sums)
    return call(
        norm_kernel,
        [((SHARD, NEAR * HEAD), BF16)],
        (y_heads, gate_input, sums, partner, norm_gain.reshape(1, -1)),
    )


def solution(mesh):
    return jax.shard_map(
        on_device,
        mesh=mesh,
        in_specs=(
            P("ctx", "tp"),
            P("ctx", "tp"),
            P("ctx", "tp"),
            P(),
            P("ctx", "tp"),
            P("ctx", None, None, None),
            P("ctx", "tp"),
            P("tp"),
            P("tp"),
            P(None, "tp"),
            P(),
            P("tp"),
        ),
        out_specs=P("ctx", "tp"),
        check_vma=False,
    )
```

profile of v0, /device:TPU:1, one launch (start us, length us, event | category | flops | bytes accessed | tf_op | source)
XLA Modules:
  0.0 104.0 jit_solution(7353446244849808208)
XLA Ops:
  0.0 0.0 copy-start
  0.0 0.0 copy-start.5
  0.0 0.8 copy-done.5
  0.8 0.0 copy-start.6
  0.8 0.8 copy-done.6
  1.6 0.9 shard_map.118
  2.5 9.0 %all-to-all-start = ((bf16[8,128,256]{2,1,0:T(8,128)(2,1)}), bf16[8,128,256]{2,1,0:T(8,128)(2,1)S(1)}, u32[]{:S(2)}, u32[]{:S(2)}) async-start(bf16[8,128,256]{2,1,0:T(8,128)(2,1)} %shard_map.118), calls=%async_computation | async-start | bytes 1048576 | tf_op jit(solution)/shard_map/all_to_all | solution.py:40
  11.6 0.0 copy-done
  11.6 0.1 constant_dynamic-slice_fusion.1
  11.7 0.0 slice-start
  11.7 0.0 copy-start.4
  11.8 0.7 slice-done
  12.5 3.3 %collective-permute-start = (bf16[16,1280]{1,0:T(8,128)(2,1)S(1)}, bf16[16,1280]{1,0:T(8,128)(2,1)S(1)}, u32[]{:S(2)}, u32[]{:S(2)}) collective-permute-start(bf16[16,1280]{1,0:T(8,128)(2,1)S(1)} %pad_maximum_fusion), channel_id=1, source_target_pairs={{0,8},{8,16},{16,24},{24,32},{32,40},{40,48},{48,56},{56,64},{64,7... | collective-permute-start | bytes 122888 | tf_op jit(solution)/shard_map/ppermute | solution.py:49
  15.9 0.7 constant_dynamic-slice_fusion
  16.6 0.1 pad_add_fusion.info
  16.7 0.0 copy-start.14
  16.7 0.7 copy-done.14
  17.4 0.1 copy.16.steps
  17.5 3.5 %collective-permute-done.rim = bf16[16,1280]{1,0:T(8,128)(2,1)S(1)} collective-permute-done((bf16[16,1280]{1,0:T(8,128)(2,1)S(1)}, bf16[16,1280]{1,0:T(8,128)(2,1)S(1)}, u32[]{:S(2)}, u32[]{:S(2)}) %collective-permute-start) | collective-permute-done | bytes 40992 | tf_op jit(solution)/shard_map/ppermute | solution.py:49
  21.0 0.0 copy-start.9
  21.0 0.0 copy-done.4
  21.0 0.7 copy-done.9
  21.7 1.8 %shard_map.119 = bf16[8,416,128]{2,1,0:T(8,128)(2,1)} custom-call(s32[4]{0:T(128)S(1)} %pad_add_fusion.info, s32[16]{0:T(128)S(1)} %copy-done.9, bf16[128,1024]{1,0:T(8,128)(2,1)S(1)} %copy-done.4, f32[128,16]{1,0:T(8,128)S(1)} %copy.16.steps, bf16[128,256]{1,0:T(8,128)(2,1)S(1)} %bitcast.19, bf16[16,1280]{1,0:T(8,128)(2,1)S(1)} %collective-permute-done.rim, ...), custom_call_target="tpu_custom_call" | custom-call | bytes 2097152 | tf_op jit(solution)/shard_map/pallas_call | solution.py:473
  23.4 5.5 %all-to-all-done = bf16[8,128,256]{2,1,0:T(8,128)(2,1)S(1)} async-done(((bf16[8,128,256]{2,1,0:T(8,128)(2,1)}), bf16[8,128,256]{2,1,0:T(8,128)(2,1)S(1)}, u32[]{:S(2)}, u32[]{:S(2)}) %all-to-all-start) | async-done | bytes 524320 | tf_op jit(solution)/shard_map/all_to_all | solution.py:40
  29.0 5.4 %all-to-all-start.1 = ((bf16[8,416,128]{2,1,0:T(8,128)(2,1)}), bf16[8,416,128]{2,1,0:T(8,128)(2,1)S(1)}, u32[]{:S(2)}, u32[]{:S(2)}) async-start(bf16[8,416,128]{2,1,0:T(8,128)(2,1)} %shard_map.119), calls=%async_computation.1 | async-start | bytes 1703936 | tf_op jit(solution)/shard_map/all_to_all | solution.py:40
  34.4 3.1 %collective-permute-start.1 = (bf16[1024,256]{1,0:T(8,128)(2,1)S(1)}, bf16[1024,256]{1,0:T(8,128)(2,1)S(1)}, u32[]{:S(2)}, u32[]{:S(2)}) collective-permute-start(bf16[1024,256]{1,0:T(8,128)(2,1)S(1)} %bitcast.15), channel_id=1, source_target_pairs={{0,64},{8,72},{16,80},{24,88},{32,96},{40,104},{48,112},{56,120},{... | collective-permute-start | bytes 1572872 | tf_op jit(solution)/shard_map/ppermute | solution.py:45
  37.5 0.7 fusion
  38.2 0.0 copy-start.10
  38.2 4.5 %collective-permute-start.2 = (bf16[512,256]{1,0:T(8,128)(2,1)}, bf16[512,256]{1,0:T(8,128)(2,1)S(1)}, u32[]{:S(2)}, u32[]{:S(2)}) collective-permute-start(bf16[512,256]{1,0:T(8,128)(2,1)} %get-tuple-element.42), channel_id=1, source_target_pairs={{0,128},{8,136},{16,144},{24,152},{32,160},{40,168},{48,176},{56,1... | collective-permute-start | bytes 786440 | tf_op jit(solution)/shard_map/ppermute | solution.py:45
  42.7 1.3 %collective-permute-start.4 = (bf16[512,256]{1,0:T(8,128)(2,1)S(1)}, bf16[512,256]{1,0:T(8,128)(2,1)S(1)}, u32[]{:S(2)}, u32[]{:S(2)}) collective-permute-start(bf16[512,256]{1,0:T(8,128)(2,1)S(1)} %get-tuple-element.41), channel_id=1, source_target_pairs={{0,192},{8,200},{16,208},{24,216},{32,224},{40,232},{48,240},{56,2... | collective-permute-start | bytes 786440 | tf_op jit(solution)/shard_map/ppermute | solution.py:45
  44.0 1.3 %collective-permute-start.3 = (bf16[512,256]{1,0:T(8,128)(2,1)S(1)}, bf16[512,256]{1,0:T(8,128)(2,1)S(1)}, u32[]{:S(2)}, u32[]{:S(2)}) collective-permute-start(bf16[512,256]{1,0:T(8,128)(2,1)S(1)} %get-tuple-element.41), channel_id=1, source_target_pairs={{0,128},{8,136},{16,144},{24,152},{32,160},{40,168},{48,176},{56,1... | collective-permute-start | bytes 786440 | tf_op jit(solution)/shard_map/ppermute | solution.py:45
  45.3 14.0 %all-to-all-done.1.received = bf16[8,416,128]{2,1,0:T(8,128)(2,1)S(1)} async-done(((bf16[8,416,128]{2,1,0:T(8,128)(2,1)}), bf16[8,416,128]{2,1,0:T(8,128)(2,1)S(1)}, u32[]{:S(2)}, u32[]{:S(2)}) %all-to-all-start.1) | async-done | bytes 852000 | tf_op jit(solution)/shard_map/all_to_all | solution.py:40
  59.3 0.0 copy-done.10
  59.3 2.1 %shard_map.120 = (f32[1024,128]{1,0:T(8,128)S(1)}, f32[16,256]{1,0:T(8,128)S(1)}, f32[1024,128]{1,0:T(8,128)S(1)}, f32[1024,128]{1,0:T(8,128)S(1)}) custom-call(s32[4]{0:T(128)S(1)} %pad_add_fusion.info, s32[16]{0:T(128)S(1)} %copy-done.9, f32[16]{0:T(128)S(1)} %copy-done.10, bf16[8,416,128]{2,1,0:T(8,128)(2,1)S(1)} %all-to-all-done.1.received), custom_call_target="tpu_custom_call" | custom-call | bytes 2097152 | tf_op jit(solution)/shard_map/pallas_call | solution.py:473
  61.5 0.0 collective-permute-done.2.back2a
  61.5 0.0 collective-permute-done.4.back3
  61.5 0.0 collective-permute-done.3.back2b
  61.5 0.0 collective-permute-done.1.back1
  61.6 0.6 collective-permute-start.5
  62.1 0.0 copy-start.7
  62.2 2.3 %shard_map.121.attended = bf16[1040,128]{1,0:T(8,128)(2,1)S(1)} custom-call(s32[4]{0:T(128)S(1)} %pad_add_fusion.info, s32[16]{0:T(128)S(1)} %copy-done.9, bf16[8,416,128]{2,1,0:T(8,128)(2,1)S(1)} %all-to-all-done.1.received, bf16[1024,256]{1,0:T(8,128)(2,1)S(1)} %bitcast.17, bf16[1024,256]{1,0:T(8,128)(2,1)S(1)} %collective-permute-done.1.back1, ...), custom_call_target="tpu_custom_call" | custom-call | flops 4294967296 | bytes 2097152 | tf_op jit(solution)/shard_map/pallas_call | solution.py:473
  64.5 0.0 collective-permute-done.5.other
  64.5 0.0 copy-start.2
  64.5 0.0 copy-done.7
  64.5 2.0 %shard_map.122 = (bf16[1024,128]{1,0:T(8,128)(2,1)S(1)}, bf16[4,128,256]{2,1,0:T(8,128)(2,1)S(1)}, bf16[4,144,256]{2,1,0:T(8,128)(2,1)}) custom-call(s32[4]{0:T(128)S(1)} %pad_add_fusion.info, bf16[1040,128]{1,0:T(8,128)(2,1)S(1)} %shard_map.121.attended, bf16[8,416,128]{2,1,0:T(8,128)(2,1)S(1)} %all-to-all-done.1.received, ...), custom_call_target="tpu_custom_call" | custom-call | bytes 2097152 | tf_op jit(solution)/shard_map/pallas_call | solution.py:473
  66.5 0.0 copy-done.2
  66.5 0.0 copy-start.11
  66.6 0.7 copy-done.11
  67.3 9.4 %all-to-all-start.2 = ((bf16[4,144,256]{2,1,0:T(8,128)(2,1)}), bf16[4,144,256]{2,1,0:T(8,128)(2,1)S(1)}, u32[]{:S(2)}, u32[]{:S(2)}) async-start(bf16[4,144,256]{2,1,0:T(8,128)(2,1)} %get-tuple-element.40), calls=%async_computation.2 | async-start | bytes 589824 | tf_op jit(solution)/shard_map/all_to_all | solution.py:582
  76.7 0.0 copy-start.13
  76.7 0.7 copy-done.13
  77.3 1.0 copy-done.3
  78.4 0.9 copy-done.12
  79.3 2.9 %shard_map.123 = (f32[1024,128]{1,0:T(8,128)S(1)}, f32[1024,128]{1,0:T(8,128)S(1)}, bf16[1024,256]{1,0:T(8,128)(2,1)S(1)}) custom-call(s32[4]{0:T(128)S(1)} %pad_add_fusion.info, s32[16]{0:T(128)S(1)} %copy-done.9, f32[16]{0:T(128)S(1)} %copy-done.10, f32[16]{0:T(128)S(1)} %copy-done.13, bf16[8,416,128]{2,1,0:T(8,128)(2,1)S(1)} %all-to-all-done.1.received, ...), custom_call_target="tpu_custom_call" | custom-call | flops 1073741824 | bytes 2097152 | tf_op jit(solution)/shard_map/pallas_call | solution.py:473
  82.2 1.3 %all-to-all-done.2.handed = bf16[4,144,256]{2,1,0:T(8,128)(2,1)S(1)} async-done(((bf16[4,144,256]{2,1,0:T(8,128)(2,1)}), bf16[4,144,256]{2,1,0:T(8,128)(2,1)S(1)}, u32[]{:S(2)}, u32[]{:S(2)}) %all-to-all-start.2) | async-done | bytes 294944 | tf_op jit(solution)/shard_map/all_to_all | solution.py:582
  83.5 0.9 shard_map.124
  84.4 0.0 copy-start.1
  84.4 14.7 %all_to_all.30.y = bf16[8,128,128]{2,1,0:T(8,128)(2,1)S(1)} all-to-all(bf16[8,128,128]{2,1,0:T(8,128)(2,1)S(1)} %bitcast.18), channel_id=1, replica_groups={{0,8,16,24,32,40,48,56},{64,72,80,88,96,104,112,120},{128,136,144,152,1..., dimensions={0} | all-to-all | bytes 524288 | tf_op jit(solution)/shard_map/all_to_all | solution.py:40
  99.1 0.0 copy-done.1
  99.1 0.3 shard_map.125.sums
  99.4 2.8 %collective-permute-start.6 = (f32[128,128]{1,0:T(8,128)S(1)}, f32[128,128]{1,0:T(8,128)S(1)}, u32[]{:S(2)}, u32[]{:S(2)}) collective-permute-start(f32[128,128]{1,0:T(8,128)S(1)} %shard_map.125.sums), channel_id=1, source_target_pairs={{0,1},{1,0},{2,3},{3,2},{4,5},{5,4},{6,7},{7,6},{8,9},{9,8},{10,11... | collective-permute-start | bytes 196616 | tf_op jit(solution)/shard_map/ppermute | solution.py:54
  102.1 0.9 collective-permute-done.6.partner
  103.0 0.0 copy-done.8
  103.0 0.9 shard_map.126
  (9 shorter events, 0.1 us)
Async XLA Ops:
  0.0 11.6 %copy-start = (bf16[128,2,4,256]{3,2,1,0:T(4,128)(2,1)S(1)}, bf16[128,2,4,256]{3,2,1,0:T(4,128)(2,1)}, u32[]{:S(2)}) copy-start(bf16[128,2,4,256]{3,2,1,0:T(4,128)(2,1)} %param.17) | copy-start | bytes 1572868
  0.0 0.8 copy-start.5
  0.8 0.8 copy-start.6
  2.5 26.4 %all-to-all-start = ((bf16[8,128,256]{2,1,0:T(8,128)(2,1)}), bf16[8,128,256]{2,1,0:T(8,128)(2,1)S(1)}, u32[]{:S(2)}, u32[]{:S(2)}) async-start(bf16[8,128,256]{2,1,0:T(8,128)(2,1)} %shard_map.118), calls=%async_computation | async-start | bytes 1048576 | tf_op jit(solution)/shard_map/all_to_all | solution.py:40
  11.7 0.8 slice-start
  11.7 9.3 %copy-start.4 = (bf16[128,1024]{1,0:T(8,128)(2,1)S(1)}, bf16[128,1024]{1,0:T(8,128)(2,1)}, u32[]{:S(2)}) copy-start(bf16[128,1024]{1,0:T(8,128)(2,1)} %queries.1) | copy-start | bytes 786436
  12.5 8.5 %collective-permute-start = (bf16[16,1280]{1,0:T(8,128)(2,1)S(1)}, bf16[16,1280]{1,0:T(8,128)(2,1)S(1)}, u32[]{:S(2)}, u32[]{:S(2)}) collective-permute-start(bf16[16,1280]{1,0:T(8,128)(2,1)S(1)} %pad_maximum_fusion), channel_id=1, source_target_pairs={{0,8},{8,16},{16,24},{24,32},{32,40},{40,48},{48,56},{56,64},{64,7... | collective-permute-start | bytes 122888 | tf_op jit(solution)/shard_map/ppermute | solution.py:49
  16.7 0.7 copy-start.14
  21.0 0.7 copy-start.9
  29.0 30.4 %all-to-all-start.1 = ((bf16[8,416,128]{2,1,0:T(8,128)(2,1)}), bf16[8,416,128]{2,1,0:T(8,128)(2,1)S(1)}, u32[]{:S(2)}, u32[]{:S(2)}) async-start(bf16[8,416,128]{2,1,0:T(8,128)(2,1)} %shard_map.119), calls=%async_computation.1 | async-start | bytes 1703936 | tf_op jit(solution)/shard_map/all_to_all | solution.py:40
  34.4 27.2 %collective-permute-start.1 = (bf16[1024,256]{1,0:T(8,128)(2,1)S(1)}, bf16[1024,256]{1,0:T(8,128)(2,1)S(1)}, u32[]{:S(2)}, u32[]{:S(2)}) collective-permute-start(bf16[1024,256]{1,0:T(8,128)(2,1)S(1)} %bitcast.15), channel_id=1, source_target_pairs={{0,64},{8,72},{16,80},{24,88},{32,96},{40,104},{48,112},{56,120},{... | collective-permute-start | bytes 1572872 | tf_op jit(solution)/shard_map/ppermute | solution.py:45
  38.2 21.1 %copy-start.10 = (f32[16]{0:T(128)S(1)}, f32[16]{0:T(128)}, u32[]{:S(2)}) copy-start(f32[16]{0:T(128)} %rates.3) | copy-start | bytes 196
  38.2 23.2 %collective-permute-start.2 = (bf16[512,256]{1,0:T(8,128)(2,1)}, bf16[512,256]{1,0:T(8,128)(2,1)S(1)}, u32[]{:S(2)}, u32[]{:S(2)}) collective-permute-start(bf16[512,256]{1,0:T(8,128)(2,1)} %get-tuple-element.42), channel_id=1, source_target_pairs={{0,128},{8,136},{16,144},{24,152},{32,160},{40,168},{48,176},{56,1... | collective-permute-start | bytes 786440 | tf_op jit(solution)/shard_map/ppermute | solution.py:45
  42.7 18.8 %collective-permute-start.4 = (bf16[512,256]{1,0:T(8,128)(2,1)S(1)}, bf16[512,256]{1,0:T(8,128)(2,1)S(1)}, u32[]{:S(2)}, u32[]{:S(2)}) collective-permute-start(bf16[512,256]{1,0:T(8,128)(2,1)S(1)} %get-tuple-element.41), channel_id=1, source_target_pairs={{0,192},{8,200},{16,208},{24,216},{32,224},{40,232},{48,240},{56,2... | collective-permute-start | bytes 786440 | tf_op jit(solution)/shard_map/ppermute | solution.py:45
  44.0 17.5 %collective-permute-start.3 = (bf16[512,256]{1,0:T(8,128)(2,1)S(1)}, bf16[512,256]{1,0:T(8,128)(2,1)S(1)}, u32[]{:S(2)}, u32[]{:S(2)}) collective-permute-start(bf16[512,256]{1,0:T(8,128)(2,1)S(1)} %get-tuple-element.41), channel_id=1, source_target_pairs={{0,128},{8,136},{16,144},{24,152},{32,160},{40,168},{48,176},{56,1... | collective-permute-start | bytes 786440 | tf_op jit(solution)/shard_map/ppermute | solution.py:45
  61.6 2.9 %collective-permute-start.5 = (bf16[8,256,128]{2,1,0:T(8,128)(2,1)S(1)}, bf16[8,256,128]{2,1,0:T(8,128)(2,1)S(1)}, u32[]{:S(2)}, u32[]{:S(2)}) collective-permute-start(bf16[8,256,128]{2,1,0:T(8,128)(2,1)S(1)} %slice.24), channel_id=1, source_target_pairs={{0,1},{1,0},{2,3},{3,2},{4,5},{5,4},{6,7},{7,6},{8,9},{9,8},{10,11... | collective-permute-start | bytes 1572872 | tf_op jit(solution)/shard_map/ppermute | solution.py:54
  62.1 2.3 %copy-start.7 = (f32[4,1024]{1,0:T(4,128)S(1)}, f32[4,1024]{1,0:T(4,128)}, u32[]{:S(2)}) copy-start(f32[4,1024]{1,0:T(4,128)} %taps.1) | copy-start | bytes 49156
  64.5 2.1 %copy-start.2 = (bf16[8,256,128]{2,1,0:T(8,128)(2,1)}, bf16[8,256,128]{2,1,0:T(8,128)(2,1)S(1)}, u32[]{:S(2)}) copy-start(bf16[8,256,128]{2,1,0:T(8,128)(2,1)S(1)} %collective-permute-done.5.other) | copy-start | bytes 1572868
  66.5 0.7 copy-start.11
  67.3 16.2 %all-to-all-start.2 = ((bf16[4,144,256]{2,1,0:T(8,128)(2,1)}), bf16[4,144,256]{2,1,0:T(8,128)(2,1)S(1)}, u32[]{:S(2)}, u32[]{:S(2)}) async-start(bf16[4,144,256]{2,1,0:T(8,128)(2,1)} %get-tuple-element.40), calls=%async_computation.2 | async-start | bytes 589824 | tf_op jit(solution)/shard_map/all_to_all | solution.py:582
  76.7 0.7 copy-start.13
  77.3 1.0 %copy-start.3 = (bf16[8,256,128]{2,1,0:T(8,128)(2,1)S(1)}, bf16[8,256,128]{2,1,0:T(8,128)(2,1)}, u32[]{:S(2)}) copy-start(bf16[8,256,128]{2,1,0:T(8,128)(2,1)} %copy-done.2) | copy-start | bytes 1572868
  78.4 0.9 copy-start.12
  84.4 14.7 %copy-start.1 = (bf16[128,1024]{1,0:T(8,128)(2,1)S(1)}, bf16[128,1024]{1,0:T(8,128)(2,1)}, u32[]{:S(2)}) copy-start(bf16[128,1024]{1,0:T(8,128)(2,1)} %gate.3) | copy-start | bytes 786436
  99.1 4.0 %copy-start.8 = (f32[1024]{0:T(1024)S(1)}, f32[1024]{0:T(1024)}, u32[]{:S(2)}) copy-start(f32[1024]{0:T(1024)} %param.23) | copy-start | bytes 12292
  99.4 3.7 %collective-permute-start.6 = (f32[128,128]{1,0:T(8,128)S(1)}, f32[128,128]{1,0:T(8,128)S(1)}, u32[]{:S(2)}, u32[]{:S(2)}) collective-permute-start(f32[128,128]{1,0:T(8,128)S(1)} %shard_map.125.sums), channel_id=1, source_target_pairs={{0,1},{1,0},{2,3},{3,2},{4,5},{5,4},{6,7},{7,6},{8,9},{9,8},{10,11... | collective-permute-start | bytes 196616 | tf_op jit(solution)/shard_map/ppermute | solution.py:54
where the time goes:
time: 105 us; the launch traced here: 104 us
  starting transfers between devices  40.7 us (39%)
  waiting for transfers between devices  25.3 us (24%)
  blocking collectives  14.7 us (14%)
  Pallas kernels  14.1 us (13%)
  local copies, waits for them, and re-layouts  8.78 us (8%)
    all_to_all x2, waiting for transfers between devices, exchange_near(): lax.all_to_all(x, 'ctx', 0, 0, axis_index_groups=near_groups(), tiled=True)  19.5 us
    all_to_all x1, blocking collectives, exchange_near(): lax.all_to_all(x, 'ctx', 0, 0, axis_index_groups=near_groups(), tiled=True)  14.7 us
    all_to_all x2, starting transfers between devices, exchange_near(): lax.all_to_all(x, 'ctx', 0, 0, axis_index_groups=near_groups(), tiled=True)  14.4 us
    pallas_call x9, Pallas kernels, call(): pl.pallas_call(kernel, out_shape=shapes[0] if single else shapes, in_spec...  14.1 us
    ppermute x4, starting transfers between devices, from_row_behind(): return lax.ppermute(x, 'ctx', pairs)  10.2 us
    all_to_all x1, starting transfers between devices, on_device(): lax.all_to_all(handed.reshape(FAR * (HEAD + 16), STATE), 'ctx', 0, 0, axi...  9.4 us
    unnamed x34, local copies, waits for them, and re-layouts  6.41 us
    ppermute x1, waiting for transfers between devices, from_shard_behind(): return lax.ppermute(x, 'ctx', [(i, i + 1) for i in range(NEAR * FAR - 1)])  3.54 us
  transfers between devices with their start and end apart: 10, of which 5 were waited for; matrix products, arithmetic and copies ran while one was open for 2% of the time, Pallas kernels for 9%

commit v1 on v0

--- a/solution.py
+++ b/solution.py
@@ -18,6 +18,7 @@
 HEAD = 128
 STATE = 256
 RIM = 16
+DOCS_AT = 4
 PAST = 10 * CHUNK
 WIDE = 256
 STEPS_AT = SHARD + RIM
@@ -54,12 +55,12 @@
     return lax.ppermute(x, "tp", [(t, t ^ 1) for t in range(count)])
 
 
-def first_tokens(docs, pos):
+def first_tokens(info, pos):
     begin = jnp.int32(0)
     first = pos
-    for d in range(docs.shape[0]):
+    for d in range(DOCS_AT, info.shape[0]):
         first = jnp.where(pos >= begin, begin, first)
-        begin = begin + docs[d]
+        begin = begin + info[d]
     return first
 
 
@@ -73,24 +74,11 @@
     return v / (1.0 + jnp.exp(-v))
 
 
-def pair_kernel(keys, values, out, sems):
-    copies = []
-    for n in range(NEAR):
-        copies.append(pltpu.make_async_copy(keys, out.at[n, :, pl.ds(0, HEAD)], sems.at[2 * n]))
-        copies.append(
-            pltpu.make_async_copy(values, out.at[n, :, pl.ds(HEAD, HEAD)], sems.at[2 * n + 1])
-        )
-    for copy in copies:
-        copy.start()
-    for copy in copies:
-        copy.wait()
-
-
-def pack_kernel(info, docs, queries, steps, raw, rim, taps, out, ext):
+def pack_kernel(info, queries, steps, raw, rim, taps, out, ext):
     ext[0:RIM] = rim[:, NEAR * HEAD :].astype(F32)
     ext[RIM:] = raw[...].astype(F32)
     pos = info[3] + lax.broadcasted_iota(jnp.int32, (1, SHARD), 1)
-    since = columns_of([(pos - first_tokens(docs, pos)).astype(F32)])[:, 0:1]
+    since = columns_of([(pos - first_tokens(info, pos)).astype(F32)])[:, 0:1]
     acc = jnp.zeros((SHARD, STATE), F32)
     for m in range(4):
         part = ext[RIM - m : RIM - m + SHARD] * taps[3 - m : 4 - m]
@@ -129,43 +117,53 @@
     rate = jnp.concatenate(
         [jnp.full((1, ROW), rates[2 * near], F32), jnp.full((1, ROW), rates[2 * near + 1], F32)], 0
     )
-    log_decay = jnp.concatenate([-rate * steps, jnp.zeros((6, ROW), F32)], 0)
+    log_decay = -rate * steps
+    stacked = jnp.concatenate(
+        [log_decay[:, k * CHUNK : (k + 1) * CHUNK] for k in range(CHUNKS)], 0
+    )
+    high = stacked.astype(BF16)
+    rest = stacked - high.astype(F32)
+    middle = rest.astype(BF16)
+    low = (rest - middle.astype(F32)).astype(BF16)
     below = lax.broadcasted_iota(jnp.int32, (CHUNK, CHUNK), 0)
     across = lax.broadcasted_iota(jnp.int32, (CHUNK, CHUNK), 1)
-    upper = jnp.where(below <= across, 1.0, 0.0).astype(F32)
-    locals_ = [
-        jnp.dot(
-            log_decay[:, k * CHUNK : (k + 1) * CHUNK],
-            upper,
-            precision=lax.Precision.HIGHEST,
-            preferred_element_type=F32,
-        )[0:2]
-        for k in range(CHUNKS)
-    ]
+    upper = jnp.where(below <= across, 1.0, 0.0).astype(BF16)
+    summed = jnp.dot(
+        jnp.concatenate([high, middle, low, jnp.zeros_like(high)], 0),
+        upper,
+        preferred_element_type=F32,
+    )
+    summed = summed[0:8] + (summed[8:16] + summed[16:24])
+    locals_ = [summed[2 * k : 2 * k + 2] for k in range(CHUNKS)]
     return locals_, [local[:, CHUNK - 1 : CHUNK] for local in locals_]
 
 
-def weights_kernel(info, docs, rates, received, weigh, decays, since, seen):
+def places_kernel(info, since, seen):
+    row_start = info[0]
+    pos = row_start + lax.broadcasted_iota(jnp.int32, (1, ROW), 1)
+    first = first_tokens(info, pos)
+    columns = columns_of([(pos - first).astype(F32), (first - row_start).astype(F32)])
+    since[...] = jnp.broadcast_to(columns[:, 0:1], (ROW, HEAD))
+    seen[...] = jnp.broadcast_to(columns[:, 1:2], (ROW, HEAD))
+
+
+def weights_kernel(info, rates, received, weigh, decays):
     steps = steps_of(received)
     locals_, totals = decays_of(steps, rates, info[1])
     row_start = info[0]
     pos = row_start + lax.broadcasted_iota(jnp.int32, (1, ROW), 1)
-    first = first_tokens(docs, pos)
-    decay_rows = []
+    first = first_tokens(info, pos)
+    rows_, decay_rows = [], []
     for k in range(CHUNKS):
         rows = slice(k * CHUNK, (k + 1) * CHUNK)
         last_start = first[:, (k + 1) * CHUNK - 1 : (k + 1) * CHUNK]
         gap = jnp.where(pos[:, rows] >= last_start, totals[k] - locals_[k], NEGATIVE_FILL)
-        w = jnp.exp(gap) * steps[:, rows]
-        begin = first[:, rows]
-        columns = columns_of(
-            [w[0:1], w[1:2], (pos[:, rows] - begin).astype(F32), (begin - row_start).astype(F32)]
-        )
-        weigh[rows] = two_heads(columns[:, 0:1], columns[:, 1:2], (CHUNK, HEAD))
-        since[rows] = jnp.broadcast_to(columns[:, 2:3], (CHUNK, HEAD))
-        seen[rows] = jnp.broadcast_to(columns[:, 3:4], (CHUNK, HEAD))
+        rows_.append(jnp.exp(gap) * steps[:, rows])
         crossing = jnp.where(last_start < row_start + k * CHUNK, jnp.exp(totals[k]), 0.0)
         decay_rows.append(jnp.broadcast_to(crossing, (2, STATE)))
+    w = jnp.concatenate(rows_, 1)
+    columns = columns_of([w[0:1], w[1:2]])
+    weigh[...] = two_heads(columns[:, 0:1], columns[:, 1:2], (ROW, HEAD))
     whole = totals[0] + totals[1] + totals[2] + totals[3]
     last = jnp.where(first[:, ROW - 1 : ROW] < row_start, jnp.exp(whole), 0.0)
     decay_rows.append(jnp.broadcast_to(last, (2, STATE)))
@@ -196,82 +194,37 @@
     return jnp.concatenate([half.reshape(CHUNK, HEAD) for half in halves], 1)
 
 
-def attend_kernel(
-    info,
-    docs,
-    received,
-    own,
-    back1,
-    back2a,
-    back2b,
-    back3,
-    seen,
-    attended,
-    top,
-    total,
-    summed,
-    halo_seen,
-    halo_top,
-    halo_total,
-    halo_summed,
-):
-    row_start = info[0]
-    halo_pos = row_start - RIM + lax.broadcasted_iota(jnp.int32, (1, HEAD), 1)
-    halo_first = columns_of([(first_tokens(docs, halo_pos) - row_start).astype(F32)])
-    halo_seen[...] = jnp.broadcast_to(halo_first[0:RIM, 0:1], (RIM, HEAD))
-    begin = jnp.int32(0)
-    cross_start, cross_end = jnp.int32(0), jnp.int32(0)
-    for d in range(docs.shape[0]):
-        inside = begin <= row_start
-        cross_start = jnp.where(inside, begin, cross_start)
-        begin = begin + docs[d]
-        cross_end = jnp.where(inside, begin, cross_end)
-    reached = cross_end - row_start
-    wide_blocks = PAST // WIDE
-    lowest = lax.div(cross_start - row_start + PAST, jnp.int32(WIDE))
-
-    def masked(raw, offset, seen_rows, diagonal):
-        count = raw.shape[0]
-        slabs = []
-        for n in range(raw.shape[1] // HEAD):
-            place = lax.broadcasted_iota(jnp.int32, (1, HEAD), 1) + (offset + n * HEAD)
-            visible = place.astype(F32) >= seen_rows
-            if diagonal is not None:
-                down = lax.broadcasted_iota(jnp.int32, (count, HEAD), 0) + diagonal
-                along = lax.broadcasted_iota(jnp.int32, (count, HEAD), 1) + n * HEAD
-                visible = visible & (along <= down)
-            slabs.append(jnp.where(visible, raw[:, n * HEAD : (n + 1) * HEAD], NEGATIVE_FILL))
-        return slabs
-
-    def largest_of(slabs):
-        most = slabs[0]
-        for slab in slabs[1:]:
-            most = jnp.maximum(most, slab)
-        return jnp.max(most, axis=1, keepdims=True)
-
-    def weighed(slabs, new_top):
-        parts, sums = [], None
-        for slab in slabs:
-            weight = jnp.exp2((slab - new_top) * EXP2_SCALE)
-            sums = weight if sums is None else sums + weight
-            parts.append(weight.astype(BF16))
-        return sums, parts
-
-    def fold(query, keys, block, within, seen_ref, top_ref, total_ref, summed_ref, rows, diagonal):
-        at = pl.ds(pl.multiple_of(within * WIDE, WIDE), WIDE)
-        raw = dot_rows(query, keys[at, 0:HEAD])
-        slabs = masked(raw, block * WIDE - PAST, seen_ref[rows], diagonal)
-        old_top = top_ref[rows]
-        new_top = jnp.maximum(old_top, largest_of(slabs))
-        factor = jnp.exp2((old_top - new_top) * EXP2_SCALE)
-        sums, parts = weighed(slabs, new_top)
-        product = jnp.dot(
-            jnp.concatenate(parts, 1), keys[at, HEAD:], preferred_element_type=F32
-        )
-        top_ref[rows] = new_top
-        total_ref[rows] = total_ref[rows] * factor + sums
-        summed_ref[rows] = summed_ref[rows] * factor + product
-
+def masked(raw, offset, seen_rows, diagonal):
+    count = raw.shape[0]
+    slabs = []
+    for n in range(raw.shape[1] // HEAD):
+        place = lax.broadcasted_iota(jnp.int32, (1, HEAD), 1) + (offset + n * HEAD)
+        visible = place.astype(F32) >= seen_rows
+        if diagonal is not None:
+            down = lax.broadcasted_iota(jnp.int32, (count, HEAD), 0) + diagonal
+            along = lax.broadcasted_iota(jnp.int32, (count, HEAD), 1) + n * HEAD
+            visible = visible & (along <= down)
+        slabs.append(jnp.where(visible, raw[:, n * HEAD : (n + 1) * HEAD], NEGATIVE_FILL))
+    return slabs
+
+
+def largest_of(slabs):
+    most = slabs[0]
+    for slab in slabs[1:]:
+        most = jnp.maximum(most, slab)
+    return jnp.max(most, axis=1, keepdims=True)
+
+
+def weighed(slabs, new_top):
+    parts, sums = [], None
+    for slab in slabs:
+        weight = jnp.exp2((slab - new_top) * EXP2_SCALE)
+        sums = weight if sums is None else sums + weight
+        parts.append(weight.astype(BF16))
+    return sums, parts
+
+
+def attend_own_kernel(received, own, seen, top, total, summed):
     raws, weights = [], [[] for _ in range(CHUNKS)]
     for j in range(CHUNKS):
         query = received[2 * j :, 0:SHARD, :].reshape(ROW - j * CHUNK, HEAD)
@@ -294,13 +247,67 @@
         product = jnp.dot(jnp.concatenate(weights[j], 0), values, preferred_element_type=F32)
         rows = slice(j * CHUNK, ROW)
         summed[rows] = product if j == 0 else summed[rows] + product
+
+
+def attend_kernel(
+    info,
+    received,
+    back1,
+    back2,
+    back3,
+    seen,
+    top_in,
+    total_in,
+    summed_in,
+    attended,
+    top,
+    total,
+    summed,
+    halo_seen,
+    halo_top,
+    halo_total,
+    halo_summed,
+):
+    row_start = info[0]
+    halo_pos = row_start - RIM + lax.broadcasted_iota(jnp.int32, (1, HEAD), 1)
+    halo_first = columns_of([(first_tokens(info, halo_pos) - row_start).astype(F32)])
+    halo_seen[...] = jnp.broadcast_to(halo_first[0:RIM, 0:1], (RIM, HEAD))
+    begin = jnp.int32(0)
+    cross_start, cross_end = jnp.int32(0), jnp.int32(0)
+    for d in range(DOCS_AT, info.shape[0]):
+        inside = begin <= row_start
+        cross_start = jnp.where(inside, begin, cross_start)
+        begin = begin + info[d]
+        cross_end = jnp.where(inside, begin, cross_end)
+    reached = cross_end - row_start
+    wide_blocks = PAST // WIDE
+    lowest = lax.div(cross_start - row_start + PAST, jnp.int32(WIDE))
+
+    def fold(query, keys, block, within, seen_ref, top_ref, total_ref, summed_ref, rows, diagonal):
+        at = pl.ds(pl.multiple_of(within * WIDE, WIDE), WIDE)
+        raw = dot_rows(query, keys[at, 0:HEAD])
+        slabs = masked(raw, block * WIDE - PAST, seen_ref[rows], diagonal)
+        old_top = top_ref[rows]
+        new_top = jnp.maximum(old_top, largest_of(slabs))
+        factor = jnp.exp2((old_top - new_top) * EXP2_SCALE)
+        sums, parts = weighed(slabs, new_top)
+        product = jnp.dot(
+            jnp.concatenate(parts, 1), keys[at, HEAD:], preferred_element_type=F32
+        )
+        top_ref[rows] = new_top
+        total_ref[rows] = total_ref[rows] * factor + sums
+        summed_ref[rows] = summed_ref[rows] * factor + product
+
+    top[...] = top_in[...]
+    total[...] = total_in[...]
+    summed[...] = summed_in[...]
     halo_top[...] = jnp.full((RIM, HEAD), NEGATIVE_FILL, F32)
     halo_total[...] = jnp.zeros((RIM, HEAD), F32)
     halo_summed[...] = jnp.zeros((RIM, HEAD), F32)
 
     def earlier(count):
         query = received[0 : 2 * count, 0:SHARD, :].reshape(count * CHUNK, HEAD)
-        for keys, begin in ((back1, 6), (back2b, 4), (back2a, 2), (back3, 0)):
+        for keys, begin in ((back1, 6), (back2, 2), (back3, 0)):
             blocks = keys.shape[0] // WIDE
 
             def visit(n, carry):
@@ -380,7 +387,7 @@
 
 
 def inner_kernel(
-    info, docs, rates, skip, received, other, x_in, states, y_out, enter_row, c_out
+    info, rates, received, other, x_in, states, y_out, enter_row, c_out
 ):
     near = info[1]
     core_zero = info[2] == 0
@@ -388,12 +395,13 @@
     locals_, totals = decays_of(steps, rates, near)
     row_start = info[0]
     pos = row_start + lax.broadcasted_iota(jnp.int32, (1, ROW), 1)
-    first = first_tokens(docs, pos)
+    first = first_tokens(info, pos)
     below = lax.broadcasted_iota(jnp.int32, (CHUNK, CHUNK), 0)
     across = lax.broadcasted_iota(jnp.int32, (CHUNK, CHUNK), 1)
     causal = across <= below
     place = across.astype(F32)
-    gain = two_heads(skip[2 * near], skip[2 * near + 1], (1, HEAD))
+    gains_at = 2 * NEAR + 2 * near
+    gain = two_heads(rates[gains_at], rates[gains_at + 1], (1, HEAD))
     shape = (CHUNK, HEAD)
     before = jnp.zeros((2, 1), F32)
     for k in range(CHUNKS):
@@ -458,7 +466,7 @@
         out[:, columns] = (gated_of(y, gate, h) * scale * gain[:, columns]).astype(BF16)
 
 
-def call(kernel, outs, args, smem=0, raw=(), raw_out=False, scratch=(), flops=0, mib=16):
+def call(kernel, outs, args, smem=0, raw=(), raw_out=False, scratch=(), flops=0, mib=8):
     specs = []
     for n in range(len(args)):
         if n < smem:
@@ -481,12 +489,12 @@
     )(*args)
 
 
-def run_attend(info, docs, received, own, back1, back2a, back2b, back3, seen):
+def run_attend(info, received, *args):
     return call(
         attend_kernel,
         [((RIM + ROW, HEAD), BF16)],
-        (info, docs, received, own, back1, back2a, back2b, back3, seen),
-        smem=2,
+        (info, received, *args),
+        smem=1,
         scratch=[
             pltpu.VMEM((ROW, HEAD), F32),
             pltpu.VMEM((ROW, HEAD), F32),
@@ -497,7 +505,7 @@
             pltpu.VMEM((RIM, HEAD), F32),
         ],
         flops=1 << 32,
-        mib=24,
+        mib=12,
     )
 
 
@@ -534,50 +542,48 @@
     near = ctx % NEAR
     core = tp % 2
     group = tp // 2
-    info = jnp.stack([(ctx // NEAR) * ROW, near, core, ctx * SHARD]).astype(jnp.int32)
+    place = jnp.stack([(ctx // NEAR) * ROW, near, core, ctx * SHARD]).astype(jnp.int32)
+    info = jnp.concatenate([place, doc_lengths])
+    rates = jnp.concatenate([decay_rate, skip_gain])
 
     bc_mine = lax.dynamic_slice(bc_input, (0, core, group, 0), (SHARD, 1, 1, STATE)).reshape(
         SHARD, STATE
     )
     taps_mine = lax.dynamic_slice(conv_bc, (0, core, group, 0), (4, 1, 1, STATE)).reshape(4, STATE)
     rim = from_shard_behind(jnp.concatenate([queries[SHARD - RIM :], bc_mine[SHARD - RIM :]], 1))
-    own = exchange_near(
-        call(
-            pair_kernel,
-            [((NEAR, SHARD, 2 * HEAD), BF16)],
-            (key_rows, value_rows),
-            raw=(0, 1),
-            raw_out=True,
-            scratch=[pltpu.SemaphoreType.DMA((2 * NEAR,))],
-        ).reshape(ROW, 2 * HEAD)
-    )
+    wide = (NEAR, SHARD, HEAD)
+    pairs = jnp.concatenate(
+        [jnp.broadcast_to(key_rows, wide), jnp.broadcast_to(value_rows, wide)], 2
+    )
+    own = exchange_near(pairs.reshape(ROW, 2 * HEAD))
+    since, seen = call(places_kernel, [((ROW, HEAD), F32)] * 2, (info,), smem=1)
     packed = call(
         pack_kernel,
         [((NEAR, PACK_ROWS, HEAD), BF16)],
-        (info, doc_lengths, queries, step_size, bc_mine, rim, taps_mine),
-        smem=2,
+        (info, queries, step_size, bc_mine, rim, taps_mine),
+        smem=1,
         scratch=[pltpu.VMEM((RIM + SHARD, STATE), F32)],
     )
     own, packed = lax.optimization_barrier((own, packed))
     half = ROW // 2
     back1 = from_row_behind(own, 1)
-    back2a = from_row_behind(own[:half], 2)
-    back2b = from_row_behind(own[half:], 2)
+    back2 = from_row_behind(own, 2)
     back3 = from_row_behind(own[half:], 3)
     received = exchange_near(packed.reshape(NEAR * PACK_ROWS, HEAD)).reshape(
         NEAR, PACK_ROWS, HEAD
     )
-    weigh, decays, since, seen = call(
+    weigh, decays = call(
         weights_kernel,
-        [((ROW, HEAD), F32), ((16, STATE), F32), ((ROW, HEAD), F32), ((ROW, HEAD), F32)],
-        (info, doc_lengths, decay_rate, received),
-        smem=3,
-    )
-    received, weigh, back1, back2a, back2b, back3 = lax.optimization_barrier(
-        (received, weigh, back1, back2a, back2b, back3)
+        [((ROW, HEAD), F32), ((16, STATE), F32)],
+        (info, rates, received),
+        smem=2,
+    )
+    own_part = call(attend_own_kernel, [((ROW, HEAD), F32)] * 3, (received, own, seen), mib=12)
+    received, weigh, back1, back2, back3, *own_part = lax.optimization_barrier(
+        (received, weigh, back1, back2, back3, *own_part)
     )
     other = with_partner(received[:, BC_AT:])
-    attended = run_attend(info, doc_lengths, received, own, back1, back2a, back2b, back3, seen)
+    attended = run_attend(info, received, back1, back2, back3, seen, *own_part)
     x, states, handed = run_scan(info, attended, received, other, conv_x, weigh, decays, since)
     handed = lax.all_to_all(
         handed.reshape(FAR * (HEAD + 16), STATE),
@@ -590,8 +596,8 @@
     y_inner, enter_row, c_row = call(
         inner_kernel,
         [((ROW, HEAD), F32), ((ROW, HEAD), F32), ((ROW, STATE), BF16)],
-        (info, doc_lengths, decay_rate, skip_gain, received, other, x, states),
-        smem=4,
+        (info, rates, received, other, x, states),
+        smem=2,
         flops=1 << 30,
     )
     y_row = call(

time: 105 us -> 101 us (0.962)
  starting transfers between devices: 40.7 us -> 37.5 us
  local copies, waits for them, and re-layouts: 8.78 us -> 6.8 us
    all_to_all x1, starting transfers between devices: 9.4 us -> 7.18 us  [on_device(): lax.all_to_all(handed.reshape(FAR * (HEAD + 16), STATE), 'ctx', 0, 0, axi...]
    unnamed x34 -> x32, local copies, waits for them, and re-layouts: 6.41 us -> 4.18 us
    ppermute x4 -> x3, starting transfers between devices: 10.2 us -> 9.8 us  [from_row_behind(): return lax.ppermute(x, 'ctx', pairs)]
    pallas_call x9 -> x10, Pallas kernels: 14.1 us -> 14.1 us  [call(): pl.pallas_call(kernel, out_shape=shapes[0] if single else shapes, in_spec...]
  transfers between devices with their start and end apart: 10 -> 9, of which waited for: 5 -> 5; matrix products, arithmetic and copies ran while one was open for 2% -> 1% of each run, Pallas kernels for 9% -> 10%
where the time goes in v1:
time: 101 us
  starting transfers between devices  37.5 us (37%)
  waiting for transfers between devices  26 us (26%)
  blocking collectives  14.9 us (15%)
  Pallas kernels  14.1 us (14%)
  local copies, waits for them, and re-layouts  6.8 us (7%)
    all_to_all x2, waiting for transfers between devices, exchange_near(): lax.all_to_all(x, 'ctx', 0, 0, axis_index_groups=near_groups(), tiled=True)  20.1 us
    all_to_all x1, blocking collectives, exchange_near(): lax.all_to_all(x, 'ctx', 0, 0, axis_index_groups=near_groups(), tiled=True)  14.9 us
    pallas_call x10, Pallas kernels, call(): pl.pallas_call(kernel, out_shape=shapes[0] if single else shapes, in_spec...  14.1 us
    all_to_all x2, starting transfers between devices, exchange_near(): lax.all_to_all(x, 'ctx', 0, 0, axis_index_groups=near_groups(), tiled=True)  13.8 us
    ppermute x3, starting transfers between devices, from_row_behind(): return lax.ppermute(x, 'ctx', pairs)  9.8 us
    all_to_all x1, starting transfers between devices, on_device(): lax.all_to_all(handed.reshape(FAR * (HEAD + 16), STATE), 'ctx', 0, 0, axi...  7.18 us
    unnamed x32, local copies, waits for them, and re-layouts  4.18 us
    ppermute x2, starting transfers between devices, with_partner(): return lax.ppermute(x, 'tp', [(t, t ^ 1) for t in range(count)])  3.36 us
  transfers between devices with their start and end apart: 9, of which 5 were waited for; matrix products, arithmetic and copies ran while one was open for 1% of the time, Pallas kernels for 10%

profile of v1, /device:TPU:1, one launch (start us, length us, event | category | flops | bytes accessed | tf_op | source)
XLA Modules:
  0.0 100.6 jit_solution(6529513239953476965)
XLA Ops:
  0.0 0.0 copy-start
  0.0 0.0 copy-start.9
  0.0 0.9 broadcast_in_dim.6
  0.9 0.0 copy-done.9
  0.9 0.9 pad_maximum_fusion
  1.8 9.0 %all-to-all-start = ((bf16[8,128,256]{2,1,0:T(8,128)(2,1)}), bf16[8,128,256]{2,1,0:T(8,128)(2,1)S(1)}, u32[]{:S(2)}, u32[]{:S(2)}) async-start(bf16[8,128,256]{2,1,0:T(8,128)(2,1)} %pad_maximum_fusion), calls=%async_computation | async-start | bytes 1048576 | tf_op jit(solution)/shard_map/all_to_all | solution.py:41
  10.8 0.0 copy-done
  10.8 0.1 constant_dynamic-slice_fusion.1
  11.0 0.0 slice-start
  11.0 0.0 copy-start.4
  11.0 0.7 slice-done
  11.7 3.3 %collective-permute-start = (bf16[16,1280]{1,0:T(8,128)(2,1)S(1)}, bf16[16,1280]{1,0:T(8,128)(2,1)S(1)}, u32[]{:S(2)}, u32[]{:S(2)}) collective-permute-start(bf16[16,1280]{1,0:T(8,128)(2,1)S(1)} %pad_maximum_fusion.1), channel_id=1, source_target_pairs={{0,8},{8,16},{16,24},{24,32},{32,40},{40,48},{48,56},{56,64},{64,7... | collective-permute-start | bytes 122888 | tf_op jit(solution)/shard_map/ppermute | solution.py:50
  15.1 0.7 constant_dynamic-slice_fusion
  15.8 0.0 copy-start.10
  15.9 0.7 copy-done.10
  16.5 0.1 copy.16.steps
  16.6 0.0 copy-start.11
  16.7 0.6 copy-done.11
  17.3 0.1 concatenate.12.info
  17.4 2.9 %collective-permute-done.rim = bf16[16,1280]{1,0:T(8,128)(2,1)S(1)} collective-permute-done((bf16[16,1280]{1,0:T(8,128)(2,1)S(1)}, bf16[16,1280]{1,0:T(8,128)(2,1)S(1)}, u32[]{:S(2)}, u32[]{:S(2)}) %collective-permute-start) | collective-permute-done | bytes 40992 | tf_op jit(solution)/shard_map/ppermute | solution.py:50
  20.3 0.0 copy-done.4
  20.3 1.8 %shard_map.118 = bf16[8,416,128]{2,1,0:T(8,128)(2,1)} custom-call(s32[20]{0:T(128)S(1)} %concatenate.12.info, bf16[128,1024]{1,0:T(8,128)(2,1)S(1)} %copy-done.4, f32[128,16]{1,0:T(8,128)S(1)} %copy.16.steps, bf16[128,256]{1,0:T(8,128)(2,1)S(1)} %bitcast.20, bf16[16,1280]{1,0:T(8,128)(2,1)S(1)} %collective-permute-done.rim, f32[4,256]{1,0:T(4,128)S(1)} %bitcast.21), custom_call_target="tpu_custom_call" | custom-call | bytes 2097152 | tf_op jit(solution)/shard_map/pallas_call | solution.py:481
  22.0 6.2 %all-to-all-done = bf16[8,128,256]{2,1,0:T(8,128)(2,1)S(1)} async-done(((bf16[8,128,256]{2,1,0:T(8,128)(2,1)}), bf16[8,128,256]{2,1,0:T(8,128)(2,1)S(1)}, u32[]{:S(2)}, u32[]{:S(2)}) %all-to-all-start) | async-done | bytes 524320 | tf_op jit(solution)/shard_map/all_to_all | solution.py:41
  28.2 4.8 %all-to-all-start.1 = ((bf16[8,416,128]{2,1,0:T(8,128)(2,1)}), bf16[8,416,128]{2,1,0:T(8,128)(2,1)S(1)}, u32[]{:S(2)}, u32[]{:S(2)}) async-start(bf16[8,416,128]{2,1,0:T(8,128)(2,1)} %shard_map.118), calls=%async_computation.1 | async-start | bytes 1703936 | tf_op jit(solution)/shard_map/all_to_all | solution.py:41
  33.0 5.5 %collective-permute-start.2 = (bf16[1024,256]{1,0:T(8,128)(2,1)S(1)}, bf16[1024,256]{1,0:T(8,128)(2,1)}, u32[]{:S(2)}, u32[]{:S(2)}) collective-permute-start(bf16[1024,256]{1,0:T(8,128)(2,1)S(1)} %bitcast.15), channel_id=1, source_target_pairs={{0,128},{8,136},{16,144},{24,152},{32,160},{40,168},{48,176},{56,1... | collective-permute-start | bytes 1572872 | tf_op jit(solution)/shard_map/ppermute | solution.py:46
  38.4 3.0 %collective-permute-start.1 = (bf16[1024,256]{1,0:T(8,128)(2,1)S(1)}, bf16[1024,256]{1,0:T(8,128)(2,1)}, u32[]{:S(2)}, u32[]{:S(2)}) collective-permute-start(bf16[1024,256]{1,0:T(8,128)(2,1)S(1)} %bitcast.16), channel_id=1, source_target_pairs={{0,64},{8,72},{16,80},{24,88},{32,96},{40,104},{48,112},{56,120},{... | collective-permute-start | bytes 1572872 | tf_op jit(solution)/shard_map/ppermute | solution.py:46
  41.5 0.0 copy-start.12
  41.5 0.0 copy-start.13
  41.5 1.3 %collective-permute-start.3 = (bf16[512,256]{1,0:T(8,128)(2,1)S(1)}, bf16[512,256]{1,0:T(8,128)(2,1)S(1)}, u32[]{:S(2)}, u32[]{:S(2)}) collective-permute-start(bf16[512,256]{1,0:T(8,128)(2,1)S(1)} %slice.18), channel_id=1, source_target_pairs={{0,192},{8,200},{16,208},{24,216},{32,224},{40,232},{48,240},{56,2... | collective-permute-start | bytes 786440 | tf_op jit(solution)/shard_map/ppermute | solution.py:46
  42.8 1.1 %shard_map.120 = (f32[1024,128]{1,0:T(8,128)S(1)}, f32[1024,128]{1,0:T(8,128)S(1)}) custom-call(s32[20]{0:T(128)S(1)} %concatenate.12.info), custom_call_target="tpu_custom_call" | custom-call | bytes 2097152 | tf_op jit(solution)/shard_map/pallas_call | solution.py:481
  43.9 0.0 copy-done.12
  43.9 0.0 copy-done.13
  43.9 0.1 pad_maximum_fusion.2.rates
  44.0 13.9 %all-to-all-done.1.received = bf16[8,416,128]{2,1,0:T(8,128)(2,1)S(1)} async-done(((bf16[8,416,128]{2,1,0:T(8,128)(2,1)}), bf16[8,416,128]{2,1,0:T(8,128)(2,1)S(1)}, u32[]{:S(2)}, u32[]{:S(2)}) %all-to-all-start.1) | async-done | bytes 852000 | tf_op jit(solution)/shard_map/all_to_all | solution.py:41
  58.0 1.3 %shard_map.119 = (f32[1024,128]{1,0:T(8,128)S(1)}, f32[16,256]{1,0:T(8,128)S(1)}) custom-call(s32[20]{0:T(128)S(1)} %concatenate.12.info, f32[32]{0:T(128)S(1)} %pad_maximum_fusion.2.rates, bf16[8,416,128]{2,1,0:T(8,128)(2,1)S(1)} %all-to-all-done.1.received), custom_call_target="tpu_custom_call" | custom-call | bytes 2097152 | tf_op jit(solution)/shard_map/pallas_call | solution.py:481
  59.3 1.5 %shard_map.121 = (f32[1024,128]{1,0:T(8,128)S(1)}, f32[1024,128]{1,0:T(8,128)S(1)}, f32[1024,128]{1,0:T(8,128)S(1)}) custom-call(bf16[8,416,128]{2,1,0:T(8,128)(2,1)S(1)} %all-to-all-done.1.received, bf16[1024,256]{1,0:T(8,128)(2,1)S(1)} %bitcast.18, f32[1024,128]{1,0:T(8,128)S(1)} %get-tuple-element.31.seen), custom_call_target="tpu_custom_call" | custom-call | bytes 2097152 | tf_op jit(solution)/shard_map/pallas_call | solution.py:481
  60.8 0.0 collective-permute-done.3.back3
  60.8 0.0 collective-permute-done.2.back2
  60.8 0.0 collective-permute-done.1.back1
  60.9 0.0 copy-start.5
  60.9 0.6 collective-permute-start.4
  61.4 1.6 %shard_map.122.attended = bf16[1040,128]{1,0:T(8,128)(2,1)S(1)} custom-call(s32[20]{0:T(128)S(1)} %concatenate.12.info, bf16[8,416,128]{2,1,0:T(8,128)(2,1)S(1)} %all-to-all-done.1.received, bf16[1024,256]{1,0:T(8,128)(2,1)} %collective-permute-done.1.back1, bf16[1024,256]{1,0:T(8,128)(2,1)} %collective-permute-done.2.back2, ...), custom_call_target="tpu_custom_call" | custom-call | flops 4294967296 | bytes 2097152 | tf_op jit(solution)/shard_map/pallas_call | solution.py:481
  63.1 0.0 collective-permute-done.4.other
  63.1 0.0 copy-start.2
  63.1 0.0 copy-done.5
  63.1 2.0 %shard_map.123 = (bf16[1024,128]{1,0:T(8,128)(2,1)S(1)}, bf16[4,128,256]{2,1,0:T(8,128)(2,1)S(1)}, bf16[4,144,256]{2,1,0:T(8,128)(2,1)}) custom-call(s32[20]{0:T(128)S(1)} %concatenate.12.info, bf16[1040,128]{1,0:T(8,128)(2,1)S(1)} %shard_map.122.attended, bf16[8,416,128]{2,1,0:T(8,128)(2,1)S(1)} %all-to-all-done.1.received, ...), custom_call_target="tpu_custom_call" | custom-call | bytes 2097152 | tf_op jit(solution)/shard_map/pallas_call | solution.py:481
  65.1 0.0 copy-done.2
  65.1 0.0 copy-start.7
  65.2 0.7 copy-done.7
  65.9 7.2 %all-to-all-start.2 = ((bf16[4,144,256]{2,1,0:T(8,128)(2,1)}), bf16[4,144,256]{2,1,0:T(8,128)(2,1)S(1)}, u32[]{:S(2)}, u32[]{:S(2)}) async-start(bf16[4,144,256]{2,1,0:T(8,128)(2,1)} %get-tuple-element.50), calls=%async_computation.2 | async-start | bytes 589824 | tf_op jit(solution)/shard_map/all_to_all | solution.py:588
  73.0 0.0 copy-start.3
  73.0 1.0 %copy-done.3 = bf16[8,256,128]{2,1,0:T(8,128)(2,1)S(1)} copy-done((bf16[8,256,128]{2,1,0:T(8,128)(2,1)S(1)}, bf16[8,256,128]{2,1,0:T(8,128)(2,1)}, u32[]{:S(2)}) %copy-start.3) | copy-done | bytes 524312
  74.1 0.9 copy-done.8
  75.0 2.7 %shard_map.124 = (f32[1024,128]{1,0:T(8,128)S(1)}, f32[1024,128]{1,0:T(8,128)S(1)}, bf16[1024,256]{1,0:T(8,128)(2,1)S(1)}) custom-call(s32[20]{0:T(128)S(1)} %concatenate.12.info, f32[32]{0:T(128)S(1)} %pad_maximum_fusion.2.rates, bf16[8,416,128]{2,1,0:T(8,128)(2,1)S(1)} %all-to-all-done.1.received, bf16[8,256,128]{2,1,0:T(8,128)(2,1)S(1)} %copy-done.3, ...), custom_call_target="tpu_custom_call" | custom-call | flops 1073741824 | bytes 2097152 | tf_op jit(solution)/shard_map/pallas_call | solution.py:481
  77.8 2.1 %all-to-all-done.2.handed = bf16[4,144,256]{2,1,0:T(8,128)(2,1)S(1)} async-done(((bf16[4,144,256]{2,1,0:T(8,128)(2,1)}), bf16[4,144,256]{2,1,0:T(8,128)(2,1)S(1)}, u32[]{:S(2)}, u32[]{:S(2)}) %all-to-all-start.2) | async-done | bytes 294944 | tf_op jit(solution)/shard_map/all_to_all | solution.py:588
  79.9 0.9 shard_map.125
  80.8 0.0 copy-start.1
  80.8 14.9 %all_to_all.30.y = bf16[8,128,128]{2,1,0:T(8,128)(2,1)S(1)} all-to-all(bf16[8,128,128]{2,1,0:T(8,128)(2,1)S(1)} %bitcast.19), channel_id=1, replica_groups={{0,8,16,24,32,40,48,56},{64,72,80,88,96,104,112,120},{128,136,144,152,1..., dimensions={0} | all-to-all | bytes 524288 | tf_op jit(solution)/shard_map/all_to_all | solution.py:41
  95.7 0.0 copy-done.1
  95.7 0.3 shard_map.126.sums
  96.0 2.8 %collective-permute-start.5 = (f32[128,128]{1,0:T(8,128)S(1)}, f32[128,128]{1,0:T(8,128)S(1)}, u32[]{:S(2)}, u32[]{:S(2)}) collective-permute-start(f32[128,128]{1,0:T(8,128)S(1)} %shard_map.126.sums), channel_id=1, source_target_pairs={{0,1},{1,0},{2,3},{3,2},{4,5},{5,4},{6,7},{7,6},{8,9},{9,8},{10,11... | collective-permute-start | bytes 196616 | tf_op jit(solution)/shard_map/ppermute | solution.py:55
  98.7 0.9 collective-permute-done.5.partner
  99.6 0.0 copy-done.6
  99.6 0.9 shard_map.127
  (10 shorter events, 0.1 us)
Async XLA Ops:
  0.0 10.8 %copy-start = (bf16[128,2,4,256]{3,2,1,0:T(4,128)(2,1)S(1)}, bf16[128,2,4,256]{3,2,1,0:T(4,128)(2,1)}, u32[]{:S(2)}) copy-start(bf16[128,2,4,256]{3,2,1,0:T(4,128)(2,1)} %param.17) | copy-start | bytes 1572868
  0.0 0.9 copy-start.9
  1.8 26.4 %all-to-all-start = ((bf16[8,128,256]{2,1,0:T(8,128)(2,1)}), bf16[8,128,256]{2,1,0:T(8,128)(2,1)S(1)}, u32[]{:S(2)}, u32[]{:S(2)}) async-start(bf16[8,128,256]{2,1,0:T(8,128)(2,1)} %pad_maximum_fusion), calls=%async_computation | async-start | bytes 1048576 | tf_op jit(solution)/shard_map/all_to_all | solution.py:41
  11.0 0.8 slice-start
  11.0 9.3 %copy-start.4 = (bf16[128,1024]{1,0:T(8,128)(2,1)S(1)}, bf16[128,1024]{1,0:T(8,128)(2,1)}, u32[]{:S(2)}) copy-start(bf16[128,1024]{1,0:T(8,128)(2,1)} %queries.1) | copy-start | bytes 786436
  11.7 8.5 %collective-permute-start = (bf16[16,1280]{1,0:T(8,128)(2,1)S(1)}, bf16[16,1280]{1,0:T(8,128)(2,1)S(1)}, u32[]{:S(2)}, u32[]{:S(2)}) collective-permute-start(bf16[16,1280]{1,0:T(8,128)(2,1)S(1)} %pad_maximum_fusion.1), channel_id=1, source_target_pairs={{0,8},{8,16},{16,24},{24,32},{32,40},{40,48},{48,56},{56,64},{64,7... | collective-permute-start | bytes 122888 | tf_op jit(solution)/shard_map/ppermute | solution.py:50
  15.8 0.7 copy-start.10
  16.6 0.7 copy-start.11
  28.2 29.7 %all-to-all-start.1 = ((bf16[8,416,128]{2,1,0:T(8,128)(2,1)}), bf16[8,416,128]{2,1,0:T(8,128)(2,1)S(1)}, u32[]{:S(2)}, u32[]{:S(2)}) async-start(bf16[8,416,128]{2,1,0:T(8,128)(2,1)} %shard_map.118), calls=%async_computation.1 | async-start | bytes 1703936 | tf_op jit(solution)/shard_map/all_to_all | solution.py:41
  33.0 27.8 %collective-permute-start.2 = (bf16[1024,256]{1,0:T(8,128)(2,1)S(1)}, bf16[1024,256]{1,0:T(8,128)(2,1)}, u32[]{:S(2)}, u32[]{:S(2)}) collective-permute-start(bf16[1024,256]{1,0:T(8,128)(2,1)S(1)} %bitcast.15), channel_id=1, source_target_pairs={{0,128},{8,136},{16,144},{24,152},{32,160},{40,168},{48,176},{56,1... | collective-permute-start | bytes 1572872 | tf_op jit(solution)/shard_map/ppermute | solution.py:46
  38.4 22.4 %collective-permute-start.1 = (bf16[1024,256]{1,0:T(8,128)(2,1)S(1)}, bf16[1024,256]{1,0:T(8,128)(2,1)}, u32[]{:S(2)}, u32[]{:S(2)}) collective-permute-start(bf16[1024,256]{1,0:T(8,128)(2,1)S(1)} %bitcast.16), channel_id=1, source_target_pairs={{0,64},{8,72},{16,80},{24,88},{32,96},{40,104},{48,112},{56,120},{... | collective-permute-start | bytes 1572872 | tf_op jit(solution)/shard_map/ppermute | solution.py:46
  41.5 2.4 %copy-start.12 = (f32[16]{0:T(128)S(1)}, f32[16]{0:T(128)}, u32[]{:S(2)}) copy-start(f32[16]{0:T(128)} %param.20) | copy-start | bytes 196
  41.5 2.4 %copy-start.13 = (f32[16]{0:T(128)S(1)}, f32[16]{0:T(128)}, u32[]{:S(2)}) copy-start(f32[16]{0:T(128)} %param.19) | copy-start | bytes 196
  41.5 19.3 %collective-permute-start.3 = (bf16[512,256]{1,0:T(8,128)(2,1)S(1)}, bf16[512,256]{1,0:T(8,128)(2,1)S(1)}, u32[]{:S(2)}, u32[]{:S(2)}) collective-permute-start(bf16[512,256]{1,0:T(8,128)(2,1)S(1)} %slice.18), channel_id=1, source_target_pairs={{0,192},{8,200},{16,208},{24,216},{32,224},{40,232},{48,240},{56,2... | collective-permute-start | bytes 786440 | tf_op jit(solution)/shard_map/ppermute | solution.py:46
  60.9 2.2 %copy-start.5 = (f32[4,1024]{1,0:T(4,128)S(1)}, f32[4,1024]{1,0:T(4,128)}, u32[]{:S(2)}) copy-start(f32[4,1024]{1,0:T(4,128)} %taps.1) | copy-start | bytes 49156
  60.9 2.2 %collective-permute-start.4 = (bf16[8,256,128]{2,1,0:T(8,128)(2,1)S(1)}, bf16[8,256,128]{2,1,0:T(8,128)(2,1)S(1)}, u32[]{:S(2)}, u32[]{:S(2)}) collective-permute-start(bf16[8,256,128]{2,1,0:T(8,128)(2,1)S(1)} %slice.19), channel_id=1, source_target_pairs={{0,1},{1,0},{2,3},{3,2},{4,5},{5,4},{6,7},{7,6},{8,9},{9,8},{10,11... | collective-permute-start | bytes 1572872 | tf_op jit(solution)/shard_map/ppermute | solution.py:55
  63.1 2.1 %copy-start.2 = (bf16[8,256,128]{2,1,0:T(8,128)(2,1)}, bf16[8,256,128]{2,1,0:T(8,128)(2,1)S(1)}, u32[]{:S(2)}) copy-start(bf16[8,256,128]{2,1,0:T(8,128)(2,1)S(1)} %collective-permute-done.4.other) | copy-start | bytes 1572868
  65.1 0.7 copy-start.7
  65.9 14.0 %all-to-all-start.2 = ((bf16[4,144,256]{2,1,0:T(8,128)(2,1)}), bf16[4,144,256]{2,1,0:T(8,128)(2,1)S(1)}, u32[]{:S(2)}, u32[]{:S(2)}) async-start(bf16[4,144,256]{2,1,0:T(8,128)(2,1)} %get-tuple-element.50), calls=%async_computation.2 | async-start | bytes 589824 | tf_op jit(solution)/shard_map/all_to_all | solution.py:588
  73.0 1.0 %copy-start.3 = (bf16[8,256,128]{2,1,0:T(8,128)(2,1)S(1)}, bf16[8,256,128]{2,1,0:T(8,128)(2,1)}, u32[]{:S(2)}) copy-start(bf16[8,256,128]{2,1,0:T(8,128)(2,1)} %copy-done.2) | copy-start | bytes 1572868
  74.1 0.9 copy-start.8
  80.8 14.9 %copy-start.1 = (bf16[128,1024]{1,0:T(8,128)(2,1)S(1)}, bf16[128,1024]{1,0:T(8,128)(2,1)}, u32[]{:S(2)}) copy-start(bf16[128,1024]{1,0:T(8,128)(2,1)} %gate.3) | copy-start | bytes 786436
  95.7 4.0 %copy-start.6 = (f32[1024]{0:T(1024)S(1)}, f32[1024]{0:T(1024)}, u32[]{:S(2)}) copy-start(f32[1024]{0:T(1024)} %param.23) | copy-start | bytes 12292
  96.0 3.7 %collective-permute-start.5 = (f32[128,128]{1,0:T(8,128)S(1)}, f32[128,128]{1,0:T(8,128)S(1)}, u32[]{:S(2)}, u32[]{:S(2)}) collective-permute-start(f32[128,128]{1,0:T(8,128)S(1)} %shard_map.126.sums), channel_id=1, source_target_pairs={{0,1},{1,0},{2,3},{3,2},{4,5},{5,4},{6,7},{7,6},{8,9},{9,8},{10,11... | collective-permute-start | bytes 196616 | tf_op jit(solution)/shard_map/ppermute | solution.py:55

commit v2 on v1

--- a/solution.py
+++ b/solution.py
@@ -138,13 +138,18 @@
     return locals_, [local[:, CHUNK - 1 : CHUNK] for local in locals_]
 
 
-def places_kernel(info, since, seen):
+def places_kernel(info, seen):
     row_start = info[0]
     pos = row_start + lax.broadcasted_iota(jnp.int32, (1, ROW), 1)
     first = first_tokens(info, pos)
-    columns = columns_of([(pos - first).astype(F32), (first - row_start).astype(F32)])
-    since[...] = jnp.broadcast_to(columns[:, 0:1], (ROW, HEAD))
-    seen[...] = jnp.broadcast_to(columns[:, 1:2], (ROW, HEAD))
+    columns = columns_of([(first - row_start).astype(F32)])
+    seen[...] = jnp.broadcast_to(columns[:, 0:1], (ROW, HEAD))
+
+
+def chunk_weights(steps, local, total, pos, last_start, chunk_start):
+    gap = jnp.where(pos >= last_start, total - local, NEGATIVE_FILL)
+    crossing = jnp.where(last_start < chunk_start, jnp.exp(total), 0.0)
+    return jnp.exp(gap) * steps, jnp.broadcast_to(crossing, (2, STATE))
 
 
 def weights_kernel(info, rates, received, weigh, decays):
@@ -157,10 +162,11 @@
     for k in range(CHUNKS):
         rows = slice(k * CHUNK, (k + 1) * CHUNK)
         last_start = first[:, (k + 1) * CHUNK - 1 : (k + 1) * CHUNK]
-        gap = jnp.where(pos[:, rows] >= last_start, totals[k] - locals_[k], NEGATIVE_FILL)
-        rows_.append(jnp.exp(gap) * steps[:, rows])
-        crossing = jnp.where(last_start < row_start + k * CHUNK, jnp.exp(totals[k]), 0.0)
-        decay_rows.append(jnp.broadcast_to(crossing, (2, STATE)))
+        w, decay = chunk_weights(
+            steps[:, rows], locals_[k], totals[k], pos[:, rows], last_start, row_start + k * CHUNK
+        )
+        rows_.append(w)
+        decay_rows.append(decay)
     w = jnp.concatenate(rows_, 1)
     columns = columns_of([w[0:1], w[1:2]])
     weigh[...] = two_heads(columns[:, 0:1], columns[:, 1:2], (ROW, HEAD))
@@ -353,7 +359,7 @@
 
 
 def scan_kernel(
-    info, attended, received, other, taps, weigh, decays, since, x_out, states, handed, ext
+    info, attended, received, other, taps, weigh, decays, seen, x_out, handed, ext
 ):
     ext[...] = attended[...].astype(F32)
     near = info[1]
@@ -363,12 +369,13 @@
     for k in range(CHUNKS):
         rows = slice(k * CHUNK, (k + 1) * CHUNK)
         acc = jnp.zeros((CHUNK, HEAD), F32)
+        place = lax.broadcasted_iota(jnp.int32, (CHUNK, HEAD), 0) + k * CHUNK
+        since = place.astype(F32) - seen[rows]
         for m in range(4):
             part = ext[RIM - m + k * CHUNK : RIM - m + (k + 1) * CHUNK] * own_taps[3 - m : 4 - m]
-            acc = acc + jnp.where(since[rows] >= m, part, 0.0)
+            acc = acc + jnp.where(since >= m, part, 0.0)
         x = silu(acc).astype(BF16)
         x_out[rows] = x
-        states[k] = state.astype(BF16)
         weighed = (x.astype(F32) * weigh[rows]).astype(BF16)
         added = lax.dot_general(
             weighed,
@@ -387,7 +394,7 @@
 
 
 def inner_kernel(
-    info, rates, received, other, x_in, states, y_out, enter_row, c_out
+    info, rates, received, other, x_in, y_out, enter_row, c_out
 ):
     near = info[1]
     core_zero = info[2] == 0
@@ -411,12 +418,17 @@
         e_chunk = jnp.exp(jnp.where(first[:, rows] < chunk_start, local, NEGATIVE_FILL))
         e_row = jnp.exp(jnp.where(first[:, rows] < row_start, before + local, NEGATIVE_FILL))
         before = before + totals[k]
-        columns = jnp.transpose(jnp.concatenate([e_chunk, e_row, local, jnp.zeros((2, CHUNK), F32)], 0))
+        last_start = first[:, (k + 1) * CHUNK - 1 : (k + 1) * CHUNK]
+        w, decay = chunk_weights(
+            steps[:, rows], local, totals[k], pos[:, rows], last_start, chunk_start
+        )
+        columns = jnp.transpose(jnp.concatenate([e_chunk, e_row, local, w], 0))
         since = columns_of([(first[:, rows] - chunk_start).astype(F32)])[:, 0:1]
         enter_row[rows] = two_heads(columns[:, 2:3], columns[:, 3:4], shape)
         c_values = chunk_of(jnp.logical_not(core_zero), received, other, k)
         c_out[rows] = c_values
-        gram = dot_rows(c_values, chunk_of(core_zero, received, other, k))
+        b_values = chunk_of(core_zero, received, other, k)
+        gram = dot_rows(c_values, b_values)
         visible = causal & (place >= since)
         x = x_in[rows]
         halves = []
@@ -427,9 +439,18 @@
         lane = lax.broadcasted_iota(jnp.int32, shape, 1)
         y = jnp.where(lane < HEAD // 2, halves[0], halves[1]) + x.astype(F32) * gain
         if k > 0:
-            carried = dot_rows(c_values, states[k])
+            carried = dot_rows(c_values, state.astype(BF16))
             y = y + two_heads(columns[:, 0:1], columns[:, 1:2], shape) * carried
         y_out[rows] = y
+        if k + 1 < CHUNKS:
+            weighed = x.astype(F32) * two_heads(columns[:, 6:7], columns[:, 7:8], shape)
+            added = lax.dot_general(
+                weighed.astype(BF16),
+                b_values,
+                (((0,), (0,)), ((), ())),
+                preferred_element_type=F32,
+            )
+            state = added if k == 0 else state * two_head_rows(decay) + added
 
 
 def carried_kernel(info, y_in, enter_row, c_in, handed, y_out):
@@ -509,15 +530,14 @@
     )
 
 
-def run_scan(info, attended, received, other, taps, weigh, decays, since):
+def run_scan(info, attended, received, other, taps, weigh, decays, seen):
     return call(
         scan_kernel,
         [
             ((ROW, HEAD), BF16),
-            ((CHUNKS, HEAD, STATE), BF16),
             ((FAR, HEAD + 16, STATE), BF16),
         ],
-        (info, attended, received, other, taps, weigh, decays, since),
+        (info, attended, received, other, taps, weigh, decays, seen),
         smem=1,
         scratch=[pltpu.VMEM((RIM + ROW, HEAD), F32)],
     )
@@ -551,12 +571,14 @@
     )
     taps_mine = lax.dynamic_slice(conv_bc, (0, core, group, 0), (4, 1, 1, STATE)).reshape(4, STATE)
     rim = from_shard_behind(jnp.concatenate([queries[SHARD - RIM :], bc_mine[SHARD - RIM :]], 1))
-    wide = (NEAR, SHARD, HEAD)
-    pairs = jnp.concatenate(
-        [jnp.broadcast_to(key_rows, wide), jnp.broadcast_to(value_rows, wide)], 2
+    wide = (NEAR, SHARD, 2 * HEAD)
+    pairs = jnp.where(
+        lax.broadcasted_iota(jnp.int32, wide, 2) < HEAD,
+        jnp.broadcast_to(jnp.pad(key_rows, ((0, 0), (0, HEAD))), wide),
+        jnp.broadcast_to(jnp.pad(value_rows, ((0, 0), (HEAD, 0))), wide),
     )
     own = exchange_near(pairs.reshape(ROW, 2 * HEAD))
-    since, seen = call(places_kernel, [((ROW, HEAD), F32)] * 2, (info,), smem=1)
+    seen = call(places_kernel, [((ROW, HEAD), F32)], (info,), smem=1)
     packed = call(
         pack_kernel,
         [((NEAR, PACK_ROWS, HEAD), BF16)],
@@ -584,7 +606,7 @@
     )
     other = with_partner(received[:, BC_AT:])
     attended = run_attend(info, received, back1, back2, back3, seen, *own_part)
-    x, states, handed = run_scan(info, attended, received, other, conv_x, weigh, decays, since)
+    x, handed = run_scan(info, attended, received, other, conv_x, weigh, decays, seen)
     handed = lax.all_to_all(
         handed.reshape(FAR * (HEAD + 16), STATE),
         "ctx",
@@ -596,7 +618,7 @@
     y_inner, enter_row, c_row = call(
         inner_kernel,
         [((ROW, HEAD), F32), ((ROW, HEAD), F32), ((ROW, STATE), BF16)],
-        (info, rates, received, other, x, states),
+        (info, rates, received, other, x),
         smem=2,
         flops=1 << 30,
     )

time: 101 us -> 100 us (0.990)
  local copies, waits for them, and re-layouts: 6.8 us -> 5.1 us
  waiting for transfers between devices: 26 us -> 27.6 us
    unnamed x32 -> x28, local copies, waits for them, and re-layouts: 4.18 us -> 2.53 us
  transfers between devices with their start and end apart: 9 -> 9, of which waited for: 5 -> 6; matrix products, arithmetic and copies ran while one was open for 1% -> 1% of each run, Pallas kernels for 10% -> 10%
where the time goes in v2:
time: 100 us; the launch traced here: 99.7 us
  starting transfers between devices  36.6 us (37%)
  waiting for transfers between devices  27.6 us (28%)
  blocking collectives  14.9 us (15%)
  Pallas kernels  14.3 us (14%)
  local copies, waits for them, and re-layouts  5.1 us (5%)
    all_to_all x2, waiting for transfers between devices, exchange_near(): lax.all_to_all(x, 'ctx', 0, 0, axis_index_groups=near_groups(), tiled=True)  21 us
    all_to_all x1, blocking collectives, exchange_near(): lax.all_to_all(x, 'ctx', 0, 0, axis_index_groups=near_groups(), tiled=True)  14.9 us
    pallas_call x10, Pallas kernels, call(): pl.pallas_call(kernel, out_shape=shapes[0] if single else shapes, in_spec...  14.3 us
    all_to_all x2, starting transfers between devices, exchange_near(): lax.all_to_all(x, 'ctx', 0, 0, axis_index_groups=near_groups(), tiled=True)  13.8 us
    ppermute x3, starting transfers between devices, from_row_behind(): return lax.ppermute(x, 'ctx', pairs)  9.02 us
    all_to_all x1, starting transfers between devices, on_device(): lax.all_to_all(handed.reshape(FAR * (HEAD + 16), STATE), 'ctx', 0, 0, axi...  7.14 us
    ppermute x2, starting transfers between devices, with_partner(): return lax.ppermute(x, 'tp', [(t, t ^ 1) for t in range(count)])  3.36 us
    ppermute x1, starting transfers between devices, from_shard_behind(): return lax.ppermute(x, 'ctx', [(i, i + 1) for i in range(NEAR * FAR - 1)])  3.34 us
  transfers between devices with their start and end apart: 9, of which 6 were waited for; matrix products, arithmetic and copies ran while one was open for 1% of the time, Pallas kernels for 10%

profile of v2, /device:TPU:1, one launch (start us, length us, event | category | flops | bytes accessed | tf_op | source)
XLA Modules:
  0.0 99.7 jit_solution(5966368603811078919)
XLA Ops:
  0.0 0.0 copy-start
  0.0 0.0 copy-start.7
  0.0 0.8 pad.8
  0.9 0.0 copy-done.7
  0.9 0.9 broadcast_select_fusion
  1.7 9.0 %all-to-all-start = ((bf16[8,128,256]{2,1,0:T(8,128)(2,1)}), bf16[8,128,256]{2,1,0:T(8,128)(2,1)S(1)}, u32[]{:S(2)}, u32[]{:S(2)}) async-start(bf16[8,128,256]{2,1,0:T(8,128)(2,1)} %broadcast_select_fusion), calls=%async_computation | async-start | bytes 1048576 | tf_op jit(solution)/shard_map/all_to_all | solution.py:41
  10.8 0.0 copy-done
  10.8 0.1 constant_dynamic-slice_fusion.1
  10.9 0.0 slice-start
  10.9 0.0 copy-start.4
  11.0 0.7 slice-done
  11.7 3.3 %collective-permute-start = (bf16[16,1280]{1,0:T(8,128)(2,1)S(1)}, bf16[16,1280]{1,0:T(8,128)(2,1)S(1)}, u32[]{:S(2)}, u32[]{:S(2)}) collective-permute-start(bf16[16,1280]{1,0:T(8,128)(2,1)S(1)} %pad_maximum_fusion), channel_id=1, source_target_pairs={{0,8},{8,16},{16,24},{24,32},{32,40},{40,48},{48,56},{56,64},{64,7... | collective-permute-start | bytes 122888 | tf_op jit(solution)/shard_map/ppermute | solution.py:50
  15.0 0.7 constant_dynamic-slice_fusion
  15.8 0.0 copy-start.8
  15.8 0.7 copy-done.8
  16.5 0.1 copy.16.steps
  16.6 0.0 copy-start.9
  16.6 0.6 copy-done.9
  17.2 0.1 concatenate.9.info
  17.3 2.9 %collective-permute-done.rim = bf16[16,1280]{1,0:T(8,128)(2,1)S(1)} collective-permute-done((bf16[16,1280]{1,0:T(8,128)(2,1)S(1)}, bf16[16,1280]{1,0:T(8,128)(2,1)S(1)}, u32[]{:S(2)}, u32[]{:S(2)}) %collective-permute-start) | collective-permute-done | bytes 40992 | tf_op jit(solution)/shard_map/ppermute | solution.py:50
  20.2 0.0 copy-done.4
  20.2 1.8 %shard_map.118 = bf16[8,416,128]{2,1,0:T(8,128)(2,1)} custom-call(s32[20]{0:T(128)S(1)} %concatenate.9.info, bf16[128,1024]{1,0:T(8,128)(2,1)S(1)} %copy-done.4, f32[128,16]{1,0:T(8,128)S(1)} %copy.16.steps, bf16[128,256]{1,0:T(8,128)(2,1)S(1)} %bitcast.20, bf16[16,1280]{1,0:T(8,128)(2,1)S(1)} %collective-permute-done.rim, f32[4,256]{1,0:T(4,128)S(1)} %bitcast.21), custom_call_target="tpu_custom_call" | custom-call | bytes 2097152 | tf_op jit(solution)/shard_map/pallas_call | solution.py:502
  22.0 6.2 %all-to-all-done = bf16[8,128,256]{2,1,0:T(8,128)(2,1)S(1)} async-done(((bf16[8,128,256]{2,1,0:T(8,128)(2,1)}), bf16[8,128,256]{2,1,0:T(8,128)(2,1)S(1)}, u32[]{:S(2)}, u32[]{:S(2)}) %all-to-all-start) | async-done | bytes 524320 | tf_op jit(solution)/shard_map/all_to_all | solution.py:41
  28.2 4.8 %all-to-all-start.1 = ((bf16[8,416,128]{2,1,0:T(8,128)(2,1)}), bf16[8,416,128]{2,1,0:T(8,128)(2,1)S(1)}, u32[]{:S(2)}, u32[]{:S(2)}) async-start(bf16[8,416,128]{2,1,0:T(8,128)(2,1)} %shard_map.118), calls=%async_computation.1 | async-start | bytes 1703936 | tf_op jit(solution)/shard_map/all_to_all | solution.py:41
  32.9 4.7 %collective-permute-start.2 = (bf16[1024,256]{1,0:T(8,128)(2,1)S(1)}, bf16[1024,256]{1,0:T(8,128)(2,1)S(1)}, u32[]{:S(2)}, u32[]{:S(2)}) collective-permute-start(bf16[1024,256]{1,0:T(8,128)(2,1)S(1)} %bitcast.15), channel_id=1, source_target_pairs={{0,128},{8,136},{16,144},{24,152},{32,160},{40,168},{48,176},{56,1... | collective-permute-start | bytes 1572872 | tf_op jit(solution)/shard_map/ppermute | solution.py:46
  37.6 3.0 %collective-permute-start.1 = (bf16[1024,256]{1,0:T(8,128)(2,1)S(1)}, bf16[1024,256]{1,0:T(8,128)(2,1)}, u32[]{:S(2)}, u32[]{:S(2)}) collective-permute-start(bf16[1024,256]{1,0:T(8,128)(2,1)S(1)} %bitcast.16), channel_id=1, source_target_pairs={{0,64},{8,72},{16,80},{24,88},{32,96},{40,104},{48,112},{56,120},{... | collective-permute-start | bytes 1572872 | tf_op jit(solution)/shard_map/ppermute | solution.py:46
  40.7 0.0 copy-start.10
  40.7 0.0 copy-start.11
  40.7 1.3 %collective-permute-start.3 = (bf16[512,256]{1,0:T(8,128)(2,1)S(1)}, bf16[512,256]{1,0:T(8,128)(2,1)S(1)}, u32[]{:S(2)}, u32[]{:S(2)}) collective-permute-start(bf16[512,256]{1,0:T(8,128)(2,1)S(1)} %slice.18), channel_id=1, source_target_pairs={{0,192},{8,200},{16,208},{24,216},{32,224},{40,232},{48,240},{56,2... | collective-permute-start | bytes 786440 | tf_op jit(solution)/shard_map/ppermute | solution.py:46
  42.0 0.9 shard_map.120.seen
  43.0 0.0 copy-done.10
  43.0 0.0 copy-done.11
  43.0 0.1 pad_maximum_fusion.1.rates
  43.0 14.9 %all-to-all-done.1.received = bf16[8,416,128]{2,1,0:T(8,128)(2,1)S(1)} async-done(((bf16[8,416,128]{2,1,0:T(8,128)(2,1)}), bf16[8,416,128]{2,1,0:T(8,128)(2,1)S(1)}, u32[]{:S(2)}, u32[]{:S(2)}) %all-to-all-start.1) | async-done | bytes 852000 | tf_op jit(solution)/shard_map/all_to_all | solution.py:41
  57.9 1.3 %shard_map.119 = (f32[1024,128]{1,0:T(8,128)S(1)}, f32[16,256]{1,0:T(8,128)S(1)}) custom-call(s32[20]{0:T(128)S(1)} %concatenate.9.info, f32[32]{0:T(128)S(1)} %pad_maximum_fusion.1.rates, bf16[8,416,128]{2,1,0:T(8,128)(2,1)S(1)} %all-to-all-done.1.received), custom_call_target="tpu_custom_call" | custom-call | bytes 2097152 | tf_op jit(solution)/shard_map/pallas_call | solution.py:502
  59.2 1.5 %shard_map.121 = (f32[1024,128]{1,0:T(8,128)S(1)}, f32[1024,128]{1,0:T(8,128)S(1)}, f32[1024,128]{1,0:T(8,128)S(1)}) custom-call(bf16[8,416,128]{2,1,0:T(8,128)(2,1)S(1)} %all-to-all-done.1.received, bf16[1024,256]{1,0:T(8,128)(2,1)S(1)} %bitcast.18, f32[1024,128]{1,0:T(8,128)S(1)} %shard_map.120.seen), custom_call_target="tpu_custom_call" | custom-call | bytes 2097152 | tf_op jit(solution)/shard_map/pallas_call | solution.py:502
  60.7 0.0 collective-permute-done.3.back3
  60.7 0.0 collective-permute-done.2.back2
  60.8 0.0 collective-permute-done.1.back1
  60.8 0.0 copy-start.5
  60.8 0.6 collective-permute-start.4
  61.4 1.5 %shard_map.122.attended = bf16[1040,128]{1,0:T(8,128)(2,1)S(1)} custom-call(s32[20]{0:T(128)S(1)} %concatenate.9.info, bf16[8,416,128]{2,1,0:T(8,128)(2,1)S(1)} %all-to-all-done.1.received, bf16[1024,256]{1,0:T(8,128)(2,1)} %collective-permute-done.1.back1, bf16[1024,256]{1,0:T(8,128)(2,1)S(1)} %collective-permute-done.2.back2, ...), custom_call_target="tpu_custom_call" | custom-call | flops 4294967296 | bytes 2097152 | tf_op jit(solution)/shard_map/pallas_call | solution.py:502
  62.9 0.1 collective-permute-done.4.other
  62.9 0.0 copy-start.2
  62.9 0.0 copy-done.5
  62.9 2.1 %shard_map.123 = (bf16[1024,128]{1,0:T(8,128)(2,1)S(1)}, bf16[4,144,256]{2,1,0:T(8,128)(2,1)}) custom-call(s32[20]{0:T(128)S(1)} %concatenate.9.info, bf16[1040,128]{1,0:T(8,128)(2,1)S(1)} %shard_map.122.attended, bf16[8,416,128]{2,1,0:T(8,128)(2,1)S(1)} %all-to-all-done.1.received, bf16[8,256,128]{2,1,0:T(8,128)(2,1)S(1)} %collective-permute-done.4.other, ...), custom_call_target="tpu_custom_call" | custom-call | bytes 2097152 | tf_op jit(solution)/shard_map/pallas_call | solution.py:502
  65.0 0.0 copy-done.2
  65.0 7.1 %all-to-all-start.2 = ((bf16[4,144,256]{2,1,0:T(8,128)(2,1)}), bf16[4,144,256]{2,1,0:T(8,128)(2,1)S(1)}, u32[]{:S(2)}, u32[]{:S(2)}) async-start(bf16[4,144,256]{2,1,0:T(8,128)(2,1)} %get-tuple-element.44), calls=%async_computation.2 | async-start | bytes 589824 | tf_op jit(solution)/shard_map/all_to_all | solution.py:610
  72.2 0.0 copy-start.3
  72.2 1.0 %copy-done.3 = bf16[8,256,128]{2,1,0:T(8,128)(2,1)S(1)} copy-done((bf16[8,256,128]{2,1,0:T(8,128)(2,1)S(1)}, bf16[8,256,128]{2,1,0:T(8,128)(2,1)}, u32[]{:S(2)}) %copy-start.3) | copy-done | bytes 524312
  73.2 3.1 %shard_map.124 = (f32[1024,128]{1,0:T(8,128)S(1)}, f32[1024,128]{1,0:T(8,128)S(1)}, bf16[1024,256]{1,0:T(8,128)(2,1)S(1)}) custom-call(s32[20]{0:T(128)S(1)} %concatenate.9.info, f32[32]{0:T(128)S(1)} %pad_maximum_fusion.1.rates, bf16[8,416,128]{2,1,0:T(8,128)(2,1)S(1)} %all-to-all-done.1.received, bf16[8,256,128]{2,1,0:T(8,128)(2,1)S(1)} %copy-done.3, ...), custom_call_target="tpu_custom_call" | custom-call | flops 1073741824 | bytes 2097152 | tf_op jit(solution)/shard_map/pallas_call | solution.py:502
  76.3 2.7 %all-to-all-done.2.handed = bf16[4,144,256]{2,1,0:T(8,128)(2,1)S(1)} async-done(((bf16[4,144,256]{2,1,0:T(8,128)(2,1)}), bf16[4,144,256]{2,1,0:T(8,128)(2,1)S(1)}, u32[]{:S(2)}, u32[]{:S(2)}) %all-to-all-start.2) | async-done | bytes 294944 | tf_op jit(solution)/shard_map/all_to_all | solution.py:610
  79.0 0.9 shard_map.125
  79.9 0.0 copy-start.1
  79.9 14.9 %all_to_all.30.y = bf16[8,128,128]{2,1,0:T(8,128)(2,1)S(1)} all-to-all(bf16[8,128,128]{2,1,0:T(8,128)(2,1)S(1)} %bitcast.19), channel_id=1, replica_groups={{0,8,16,24,32,40,48,56},{64,72,80,88,96,104,112,120},{128,136,144,152,1..., dimensions={0} | all-to-all | bytes 524288 | tf_op jit(solution)/shard_map/all_to_all | solution.py:41
  94.8 0.0 copy-done.1
  94.8 0.0 copy-start.6
  94.8 0.3 shard_map.126.sums
  95.1 2.8 %collective-permute-start.5 = (f32[128,128]{1,0:T(8,128)S(1)}, f32[128,128]{1,0:T(8,128)S(1)}, u32[]{:S(2)}, u32[]{:S(2)}) collective-permute-start(f32[128,128]{1,0:T(8,128)S(1)} %shard_map.126.sums), channel_id=1, source_target_pairs={{0,1},{1,0},{2,3},{3,2},{4,5},{5,4},{6,7},{7,6},{8,9},{9,8},{10,11... | collective-permute-start | bytes 196616 | tf_op jit(solution)/shard_map/ppermute | solution.py:55
  97.9 0.9 collective-permute-done.5.partner
  98.8 0.0 copy-done.6
  98.8 0.9 shard_map.127
  (9 shorter events, 0.1 us)
Async XLA Ops:
  0.0 10.8 %copy-start = (bf16[128,2,4,256]{3,2,1,0:T(4,128)(2,1)S(1)}, bf16[128,2,4,256]{3,2,1,0:T(4,128)(2,1)}, u32[]{:S(2)}) copy-start(bf16[128,2,4,256]{3,2,1,0:T(4,128)(2,1)} %param.17) | copy-start | bytes 1572868
  0.0 0.8 copy-start.7
  1.7 26.4 %all-to-all-start = ((bf16[8,128,256]{2,1,0:T(8,128)(2,1)}), bf16[8,128,256]{2,1,0:T(8,128)(2,1)S(1)}, u32[]{:S(2)}, u32[]{:S(2)}) async-start(bf16[8,128,256]{2,1,0:T(8,128)(2,1)} %broadcast_select_fusion), calls=%async_computation | async-start | bytes 1048576 | tf_op jit(solution)/shard_map/all_to_all | solution.py:41
  10.9 0.8 slice-start
  10.9 9.3 %copy-start.4 = (bf16[128,1024]{1,0:T(8,128)(2,1)S(1)}, bf16[128,1024]{1,0:T(8,128)(2,1)}, u32[]{:S(2)}) copy-start(bf16[128,1024]{1,0:T(8,128)(2,1)} %queries.1) | copy-start | bytes 786436
  11.7 8.5 %collective-permute-start = (bf16[16,1280]{1,0:T(8,128)(2,1)S(1)}, bf16[16,1280]{1,0:T(8,128)(2,1)S(1)}, u32[]{:S(2)}, u32[]{:S(2)}) collective-permute-start(bf16[16,1280]{1,0:T(8,128)(2,1)S(1)} %pad_maximum_fusion), channel_id=1, source_target_pairs={{0,8},{8,16},{16,24},{24,32},{32,40},{40,48},{48,56},{56,64},{64,7... | collective-permute-start | bytes 122888 | tf_op jit(solution)/shard_map/ppermute | solution.py:50
  15.8 0.7 copy-start.8
  16.6 0.7 copy-start.9
  28.2 29.7 %all-to-all-start.1 = ((bf16[8,416,128]{2,1,0:T(8,128)(2,1)}), bf16[8,416,128]{2,1,0:T(8,128)(2,1)S(1)}, u32[]{:S(2)}, u32[]{:S(2)}) async-start(bf16[8,416,128]{2,1,0:T(8,128)(2,1)} %shard_map.118), calls=%async_computation.1 | async-start | bytes 1703936 | tf_op jit(solution)/shard_map/all_to_all | solution.py:41
  32.9 27.8 %collective-permute-start.2 = (bf16[1024,256]{1,0:T(8,128)(2,1)S(1)}, bf16[1024,256]{1,0:T(8,128)(2,1)S(1)}, u32[]{:S(2)}, u32[]{:S(2)}) collective-permute-start(bf16[1024,256]{1,0:T(8,128)(2,1)S(1)} %bitcast.15), channel_id=1, source_target_pairs={{0,128},{8,136},{16,144},{24,152},{32,160},{40,168},{48,176},{56,1... | collective-permute-start | bytes 1572872 | tf_op jit(solution)/shard_map/ppermute | solution.py:46
  37.6 23.2 %collective-permute-start.1 = (bf16[1024,256]{1,0:T(8,128)(2,1)S(1)}, bf16[1024,256]{1,0:T(8,128)(2,1)}, u32[]{:S(2)}, u32[]{:S(2)}) collective-permute-start(bf16[1024,256]{1,0:T(8,128)(2,1)S(1)} %bitcast.16), channel_id=1, source_target_pairs={{0,64},{8,72},{16,80},{24,88},{32,96},{40,104},{48,112},{56,120},{... | collective-permute-start | bytes 1572872 | tf_op jit(solution)/shard_map/ppermute | solution.py:46
  40.7 2.3 %copy-start.10 = (f32[16]{0:T(128)S(1)}, f32[16]{0:T(128)}, u32[]{:S(2)}) copy-start(f32[16]{0:T(128)} %param.20) | copy-start | bytes 196
  40.7 2.3 %copy-start.11 = (f32[16]{0:T(128)S(1)}, f32[16]{0:T(128)}, u32[]{:S(2)}) copy-start(f32[16]{0:T(128)} %param.19) | copy-start | bytes 196
  40.7 20.0 %collective-permute-start.3 = (bf16[512,256]{1,0:T(8,128)(2,1)S(1)}, bf16[512,256]{1,0:T(8,128)(2,1)S(1)}, u32[]{:S(2)}, u32[]{:S(2)}) collective-permute-start(bf16[512,256]{1,0:T(8,128)(2,1)S(1)} %slice.18), channel_id=1, source_target_pairs={{0,192},{8,200},{16,208},{24,216},{32,224},{40,232},{48,240},{56,2... | collective-permute-start | bytes 786440 | tf_op jit(solution)/shard_map/ppermute | solution.py:46
  60.8 2.1 %copy-start.5 = (f32[4,1024]{1,0:T(4,128)S(1)}, f32[4,1024]{1,0:T(4,128)}, u32[]{:S(2)}) copy-start(f32[4,1024]{1,0:T(4,128)} %taps.1) | copy-start | bytes 49156
  60.8 2.1 %collective-permute-start.4 = (bf16[8,256,128]{2,1,0:T(8,128)(2,1)S(1)}, bf16[8,256,128]{2,1,0:T(8,128)(2,1)S(1)}, u32[]{:S(2)}, u32[]{:S(2)}) collective-permute-start(bf16[8,256,128]{2,1,0:T(8,128)(2,1)S(1)} %slice.19), channel_id=1, source_target_pairs={{0,1},{1,0},{2,3},{3,2},{4,5},{5,4},{6,7},{7,6},{8,9},{9,8},{10,11... | collective-permute-start | bytes 1572872 | tf_op jit(solution)/shard_map/ppermute | solution.py:55
  62.9 2.1 %copy-start.2 = (bf16[8,256,128]{2,1,0:T(8,128)(2,1)}, bf16[8,256,128]{2,1,0:T(8,128)(2,1)S(1)}, u32[]{:S(2)}) copy-start(bf16[8,256,128]{2,1,0:T(8,128)(2,1)S(1)} %collective-permute-done.4.other) | copy-start | bytes 1572868
  65.0 14.0 %all-to-all-start.2 = ((bf16[4,144,256]{2,1,0:T(8,128)(2,1)}), bf16[4,144,256]{2,1,0:T(8,128)(2,1)S(1)}, u32[]{:S(2)}, u32[]{:S(2)}) async-start(bf16[4,144,256]{2,1,0:T(8,128)(2,1)} %get-tuple-element.44), calls=%async_computation.2 | async-start | bytes 589824 | tf_op jit(solution)/shard_map/all_to_all | solution.py:610
  72.2 1.0 %copy-start.3 = (bf16[8,256,128]{2,1,0:T(8,128)(2,1)S(1)}, bf16[8,256,128]{2,1,0:T(8,128)(2,1)}, u32[]{:S(2)}) copy-start(bf16[8,256,128]{2,1,0:T(8,128)(2,1)} %copy-done.2) | copy-start | bytes 1572868
  79.9 14.9 %copy-start.1 = (bf16[128,1024]{1,0:T(8,128)(2,1)S(1)}, bf16[128,1024]{1,0:T(8,128)(2,1)}, u32[]{:S(2)}) copy-start(bf16[128,1024]{1,0:T(8,128)(2,1)} %gate.3) | copy-start | bytes 786436
  94.8 4.0 %copy-start.6 = (f32[1024]{0:T(1024)S(1)}, f32[1024]{0:T(1024)}, u32[]{:S(2)}) copy-start(f32[1024]{0:T(1024)} %param.23) | copy-start | bytes 12292
  95.1 3.7 %collective-permute-start.5 = (f32[128,128]{1,0:T(8,128)S(1)}, f32[128,128]{1,0:T(8,128)S(1)}, u32[]{:S(2)}, u32[]{:S(2)}) collective-permute-start(f32[128,128]{1,0:T(8,128)S(1)} %shard_map.126.sums), channel_id=1, source_target_pairs={{0,1},{1,0},{2,3},{3,2},{4,5},{5,4},{6,7},{7,6},{8,9},{9,8},{10,11... | collective-permute-start | bytes 196616 | tf_op jit(solution)/shard_map/ppermute | solution.py:55

commit v3 on v2

--- a/solution.py
+++ b/solution.py
@@ -21,9 +21,11 @@
 DOCS_AT = 4
 PAST = 10 * CHUNK
 WIDE = 256
-STEPS_AT = SHARD + RIM
-BC_AT = STEPS_AT + 16
-PACK_ROWS = BC_AT + 2 * SHARD
+STEPS_AT = SHARD
+BC_AT = STEPS_AT + RIM
+SIDE_AT = BC_AT + 2 * SHARD
+SIDE = 16
+PACK_ROWS = SIDE_AT + 2 * SIDE
 EXP2_SCALE = math.log2(math.e) / math.sqrt(HEAD)
 F32 = jnp.float32
 BF16 = jnp.bfloat16
@@ -74,7 +76,7 @@
     return v / (1.0 + jnp.exp(-v))
 
 
-def pack_kernel(info, queries, steps, raw, rim, taps, out, ext):
+def pack_kernel(info, queries, steps, raw, rim, taps, side, out, ext):
     ext[0:RIM] = rim[:, NEAR * HEAD :].astype(F32)
     ext[RIM:] = raw[...].astype(F32)
     pos = info[3] + lax.broadcasted_iota(jnp.int32, (1, SHARD), 1)
@@ -92,12 +94,13 @@
     for n in range(NEAR):
         out[n, 0:SHARD] = queries[:, n * HEAD : (n + 1) * HEAD]
         two = slice(2 * n, 2 * n + 2)
-        out[n, SHARD:STEPS_AT] = rim[:, n * HEAD : (n + 1) * HEAD]
+        behind = rim[:, n * HEAD : (n + 1) * HEAD].astype(F32)
         out[n, STEPS_AT:BC_AT] = jnp.concatenate(
-            [high[two], middle[two], low[two], jnp.zeros((10, HEAD), F32)], 0
+            [high[two], middle[two], low[two], jnp.zeros((2, HEAD), F32), behind[RIM // 2 :]], 0
         ).astype(BF16)
         out[n, BC_AT : BC_AT + SHARD] = convolved[:, 0:HEAD]
-        out[n, BC_AT + SHARD :] = convolved[:, HEAD:]
+        out[n, BC_AT + SHARD : SIDE_AT] = convolved[:, HEAD:]
+        out[n, SIDE_AT:] = side[...]
 
 
 def two_heads(first, second, shape):
@@ -200,11 +203,16 @@
     return jnp.concatenate([half.reshape(CHUNK, HEAD) for half in halves], 1)
 
 
-def masked(raw, offset, seen_rows, diagonal):
+def masked(raw, offset, seen_rows, diagonal, halved=False):
     count = raw.shape[0]
     slabs = []
     for n in range(raw.shape[1] // HEAD):
-        place = lax.broadcasted_iota(jnp.int32, (1, HEAD), 1) + (offset + n * HEAD)
+        place = lax.broadcasted_iota(jnp.int32, (1, HEAD), 1) + n * HEAD
+        if halved:
+            rest = jnp.where(place < SHARD + SIDE, place - SIDE, place)
+            first = jnp.where(place < SIDE, place, place + (SHARD - SIDE))
+            place = jnp.where(place < 2 * SIDE, first, rest)
+        place = place + offset
         visible = place.astype(F32) >= seen_rows
         if diagonal is not None:
             down = lax.broadcasted_iota(jnp.int32, (count, HEAD), 0) + diagonal
@@ -289,16 +297,30 @@
     wide_blocks = PAST // WIDE
     lowest = lax.div(cross_start - row_start + PAST, jnp.int32(WIDE))
 
-    def fold(query, keys, block, within, seen_ref, top_ref, total_ref, summed_ref, rows, diagonal):
+    def keys_of(back, within):
         at = pl.ds(pl.multiple_of(within * WIDE, WIDE), WIDE)
-        raw = dot_rows(query, keys[at, 0:HEAD])
-        slabs = masked(raw, block * WIDE - PAST, seen_ref[rows], diagonal)
+        return back[at, 0:HEAD], back[at, HEAD:]
+
+    def halved_keys_of(back, within):
+        two = pl.ds(2 * within, 2)
+        first = received[two, SIDE_AT : SIDE_AT + SIDE, :], received[two, SIDE_AT + SIDE :, :]
+        second = back[two, :, 0:HEAD], back[two, :, HEAD:]
+        return [
+            jnp.concatenate([x.reshape(-1, HEAD), y.reshape(-1, HEAD)], 0)
+            for x, y in zip(first, second)
+        ]
+
+    def fold(
+        query, keys, values, block, seen_ref, top_ref, total_ref, summed_ref, rows, diagonal, halved
+    ):
+        raw = dot_rows(query, keys)
+        slabs = masked(raw, block * WIDE - PAST, seen_ref[rows], diagonal, halved)
         old_top = top_ref[rows]
         new_top = jnp.maximum(old_top, largest_of(slabs))
         factor = jnp.exp2((old_top - new_top) * EXP2_SCALE)
         sums, parts = weighed(slabs, new_top)
         product = jnp.dot(
-            jnp.concatenate(parts, 1), keys[at, HEAD:], preferred_element_type=F32
+            jnp.concatenate(parts, 1), values, preferred_element_type=F32
         )
         top_ref[rows] = new_top
         total_ref[rows] = total_ref[rows] * factor + sums
@@ -311,28 +333,42 @@
     halo_total[...] = jnp.zeros((RIM, HEAD), F32)
     halo_summed[...] = jnp.zeros((RIM, HEAD), F32)
 
+    halo_query = received[0, STEPS_AT:BC_AT]
+
     def earlier(count):
         query = received[0 : 2 * count, 0:SHARD, :].reshape(count * CHUNK, HEAD)
-        for keys, begin in ((back1, 6), (back2, 2), (back3, 0)):
-            blocks = keys.shape[0] // WIDE
+        for back, begin, blocks in ((back1, 6, 4), (back2, 2, 4), (back3, 0, 2)):
+            halved = back is back2
 
             def visit(n, carry):
                 within = blocks - 1 - n
                 block = begin + within
+                keys, values = (halved_keys_of if halved else keys_of)(back, within)
                 fold(
-                    query, keys, block, within, seen, top, total, summed, slice(0, count * CHUNK), None
+                    query,
+                    keys,
+                    values,
+                    block,
+                    seen,
+                    top,
+                    total,
+                    summed,
+                    slice(0, count * CHUNK),
+                    None,
+                    halved,
                 )
                 fold(
-                    received[0, SHARD:STEPS_AT],
+                    halo_query,
                     keys,
+                    values,
                     block,
-                    within,
                     halo_seen,
                     halo_top,
                     halo_total,
                     halo_summed,
                     slice(0, RIM),
-                    (PAST - RIM) - block * WIDE,
+                    (PAST - RIM) - block * WIDE if back is back1 else None,
+                    halved,
                 )
                 return carry
 
@@ -487,7 +523,7 @@
         out[:, columns] = (gated_of(y, gate, h) * scale * gain[:, columns]).astype(BF16)
 
 
-def call(kernel, outs, args, smem=0, raw=(), raw_out=False, scratch=(), flops=0, mib=8):
+def call(kernel, outs, args, smem=0, raw=(), raw_out=False, scratch=(), flops=0, mib=4):
     specs = []
     for n in range(len(args)):
         if n < smem:
@@ -526,7 +562,7 @@
             pltpu.VMEM((RIM, HEAD), F32),
         ],
         flops=1 << 32,
-        mib=12,
+        mib=7,
     )
 
 
@@ -577,19 +613,20 @@
         jnp.broadcast_to(jnp.pad(key_rows, ((0, 0), (0, HEAD))), wide),
         jnp.broadcast_to(jnp.pad(value_rows, ((0, 0), (HEAD, 0))), wide),
     )
+    side = from_row_behind(jnp.concatenate([key_rows[:SIDE], value_rows[:SIDE]], 0), 2)
     own = exchange_near(pairs.reshape(ROW, 2 * HEAD))
     seen = call(places_kernel, [((ROW, HEAD), F32)], (info,), smem=1)
     packed = call(
         pack_kernel,
         [((NEAR, PACK_ROWS, HEAD), BF16)],
-        (info, queries, step_size, bc_mine, rim, taps_mine),
+        (info, queries, step_size, bc_mine, rim, taps_mine, side),
         smem=1,
         scratch=[pltpu.VMEM((RIM + SHARD, STATE), F32)],
     )
     own, packed = lax.optimization_barrier((own, packed))
     half = ROW // 2
     back1 = from_row_behind(own, 1)
-    back2 = from_row_behind(own, 2)
+    back2 = from_row_behind(own.reshape(NEAR, SHARD, 2 * HEAD)[:, SIDE:], 2)
     back3 = from_row_behind(own[half:], 3)
     received = exchange_near(packed.reshape(NEAR * PACK_ROWS, HEAD)).reshape(
         NEAR, PACK_ROWS, HEAD
@@ -600,11 +637,11 @@
         (info, rates, received),
         smem=2,
     )
-    own_part = call(attend_own_kernel, [((ROW, HEAD), F32)] * 3, (received, own, seen), mib=12)
+    own_part = call(attend_own_kernel, [((ROW, HEAD), F32)] * 3, (received, own, seen), mib=7)
     received, weigh, back1, back2, back3, *own_part = lax.optimization_barrier(
         (received, weigh, back1, back2, back3, *own_part)
     )
-    other = with_partner(received[:, BC_AT:])
+    other = with_partner(received[:, BC_AT:SIDE_AT])
     attended = run_attend(info, received, back1, back2, back3, seen, *own_part)
     x, handed = run_scan(info, attended, received, other, conv_x, weigh, decays, seen)
     handed = lax.all_to_all(

time: 100 us -> 101 us (1.010)
  starting transfers between devices: 36.6 us -> 43.7 us
  waiting for transfers between devices: 27.6 us -> 21.6 us
  local copies, waits for them, and re-layouts: 5.1 us -> 6.6 us
  blocking collectives: 14.9 us -> 13.8 us
    ppermute x3 -> x4, starting transfers between devices: 9.02 us -> 14.2 us  [from_row_behind(): return lax.ppermute(x, 'ctx', pairs)]
    all_to_all x2, waiting for transfers between devices: 21 us -> 17.8 us  [exchange_near(): lax.all_to_all(x, 'ctx', 0, 0, axis_index_groups=near_groups(), tiled=True)]
    ppermute x1, waiting for transfers between devices: 2.88 us -> 0.01 us  [from_shard_behind(): return lax.ppermute(x, 'ctx', [(i, i + 1) for i in range(NEAR * FAR - 1)])]
    all_to_all x1, starting transfers between devices: 7.14 us -> 8.98 us  [on_device(): lax.all_to_all(handed.reshape(FAR * (HEAD + 16), STATE), 'ctx', 0, 0, axi...]
    slice x1 -> x6, local copies, waits for them, and re-layouts: 0.04 us -> 1.54 us  [the longest x1 0.81 us: on_device(): back2 = from_row_behind(own.reshape(NEAR, SHARD, 2 * HEAD)[:, SIDE:], 2)]
    all_to_all x1, blocking collectives: 14.9 us -> 13.8 us  [exchange_near(): lax.all_to_all(x, 'ctx', 0, 0, axis_index_groups=near_groups(), tiled=True)]
  transfers between devices with their start and end apart: 9 -> 10, of which waited for: 6 -> 5; matrix products, arithmetic and copies ran while one was open for 1% -> 2% of each run, Pallas kernels for 10% -> 10%
where the time goes in v3:
time: 101 us
  starting transfers between devices  43.7 us (43%)
  waiting for transfers between devices  21.6 us (21%)
  Pallas kernels  14.2 us (14%)
  blocking collectives  13.8 us (14%)
  local copies, waits for them, and re-layouts  6.6 us (7%)
    all_to_all x2, waiting for transfers between devices, exchange_near(): lax.all_to_all(x, 'ctx', 0, 0, axis_index_groups=near_groups(), tiled=True)  17.8 us
    ppermute x4, starting transfers between devices, from_row_behind(): return lax.ppermute(x, 'ctx', pairs)  14.2 us
    pallas_call x10, Pallas kernels, call(): pl.pallas_call(kernel, out_shape=shapes[0] if single else shapes, in_spec...  14.2 us
    all_to_all x1, blocking collectives, exchange_near(): lax.all_to_all(x, 'ctx', 0, 0, axis_index_groups=near_groups(), tiled=True)  13.8 us
    all_to_all x2, starting transfers between devices, exchange_near(): lax.all_to_all(x, 'ctx', 0, 0, axis_index_groups=near_groups(), tiled=True)  13.8 us
    all_to_all x1, starting transfers between devices, on_device(): lax.all_to_all(handed.reshape(FAR * (HEAD + 16), STATE), 'ctx', 0, 0, axi...  8.98 us
    ppermute x1, starting transfers between devices, from_shard_behind(): return lax.ppermute(x, 'ctx', [(i, i + 1) for i in range(NEAR * FAR - 1)])  3.36 us
    ppermute x2, starting transfers between devices, with_partner(): return lax.ppermute(x, 'tp', [(t, t ^ 1) for t in range(count)])  3.35 us
  transfers between devices with their start and end apart: 10, of which 5 were waited for; matrix products, arithmetic and copies ran while one was open for 2% of the time, Pallas kernels for 10%

profile of v3, /device:TPU:1, one launch (start us, length us, event | category | flops | bytes accessed | tf_op | source)
XLA Modules:
  0.0 101.1 jit_solution(5151881981995900044)
XLA Ops:
  0.0 0.0 copy-start
  0.0 0.0 copy-start.7
  0.0 0.8 pad.8
  0.9 0.0 copy-done.7
  0.9 0.8 broadcast_select_fusion
  1.7 9.0 %all-to-all-start = ((bf16[8,128,256]{2,1,0:T(8,128)(2,1)}), bf16[8,128,256]{2,1,0:T(8,128)(2,1)S(1)}, u32[]{:S(2)}, u32[]{:S(2)}) async-start(bf16[8,128,256]{2,1,0:T(8,128)(2,1)} %broadcast_select_fusion), calls=%async_computation | async-start | bytes 1048576 | tf_op jit(solution)/shard_map/all_to_all | solution.py:43
  10.7 0.0 slice-start.2
  10.7 0.7 slice-done.1
  11.4 0.0 slice-done.2
  11.4 4.6 %collective-permute-start.1 = (bf16[32,128]{1,0:T(8,128)(2,1)S(1)}, bf16[32,128]{1,0:T(8,128)(2,1)S(1)}, u32[]{:S(2)}, u32[]{:S(2)}) collective-permute-start(bf16[32,128]{1,0:T(8,128)(2,1)S(1)} %pad_maximum_fusion.1), channel_id=1, source_target_pairs={{0,128},{8,136},{16,144},{24,152},{32,160},{40,168},{48,176},{56,1... | collective-permute-start | bytes 24584 | tf_op jit(solution)/shard_map/ppermute | solution.py:48
  16.1 0.0 copy-done
  16.1 0.1 constant_dynamic-slice_fusion.1
  16.3 0.0 slice-start
  16.3 0.0 copy-start.4
  16.3 0.7 slice-done
  17.0 3.4 %collective-permute-start = (bf16[16,1280]{1,0:T(8,128)(2,1)S(1)}, bf16[16,1280]{1,0:T(8,128)(2,1)S(1)}, u32[]{:S(2)}, u32[]{:S(2)}) collective-permute-start(bf16[16,1280]{1,0:T(8,128)(2,1)S(1)} %pad_maximum_fusion), channel_id=1, source_target_pairs={{0,8},{8,16},{16,24},{24,32},{32,40},{40,48},{48,56},{56,64},{64,7... | collective-permute-start | bytes 122888 | tf_op jit(solution)/shard_map/ppermute | solution.py:52
  20.4 0.7 constant_dynamic-slice_fusion
  21.1 0.0 copy-start.8
  21.2 0.7 copy-done.8
  21.8 0.1 copy.16.steps
  22.0 0.0 copy-start.9
  22.0 0.6 copy-done.9
  22.6 0.1 concatenate.12.info
  22.7 0.0 collective-permute-done.1.side
  22.7 0.0 collective-permute-done.rim
  22.7 0.0 copy-done.4
  22.7 1.8 %shard_map.118 = bf16[8,432,128]{2,1,0:T(8,128)(2,1)} custom-call(s32[20]{0:T(128)S(1)} %concatenate.12.info, bf16[128,1024]{1,0:T(8,128)(2,1)S(1)} %copy-done.4, f32[128,16]{1,0:T(8,128)S(1)} %copy.16.steps, bf16[128,256]{1,0:T(8,128)(2,1)S(1)} %bitcast.20, bf16[16,1280]{1,0:T(8,128)(2,1)S(1)} %collective-permute-done.rim, f32[4,256]{1,0:T(4,128)S(1)} %bitcast.21, ...), custom_call_target="tpu_custom_call" | custom-call | bytes 2097152 | tf_op jit(solution)/shard_map/pallas_call | solution.py:538
  24.5 3.7 %all-to-all-done = bf16[8,128,256]{2,1,0:T(8,128)(2,1)S(1)} async-done(((bf16[8,128,256]{2,1,0:T(8,128)(2,1)}), bf16[8,128,256]{2,1,0:T(8,128)(2,1)S(1)}, u32[]{:S(2)}, u32[]{:S(2)}) %all-to-all-start) | async-done | bytes 524320 | tf_op jit(solution)/shard_map/all_to_all | solution.py:43
  28.1 4.8 %all-to-all-start.1 = ((bf16[8,432,128]{2,1,0:T(8,128)(2,1)}), bf16[8,432,128]{2,1,0:T(8,128)(2,1)S(1)}, u32[]{:S(2)}, u32[]{:S(2)}) async-start(bf16[8,432,128]{2,1,0:T(8,128)(2,1)} %shard_map.118), calls=%async_computation.1 | async-start | bytes 1769472 | tf_op jit(solution)/shard_map/all_to_all | solution.py:43
  32.9 3.1 %collective-permute-start.2 = (bf16[1024,256]{1,0:T(8,128)(2,1)S(1)}, bf16[1024,256]{1,0:T(8,128)(2,1)S(1)}, u32[]{:S(2)}, u32[]{:S(2)}) collective-permute-start(bf16[1024,256]{1,0:T(8,128)(2,1)S(1)} %bitcast.16), channel_id=1, source_target_pairs={{0,64},{8,72},{16,80},{24,88},{32,96},{40,104},{48,112},{56,120},{... | collective-permute-start | bytes 1572872 | tf_op jit(solution)/shard_map/ppermute | solution.py:48
  36.0 0.8 slice.33
  36.8 5.1 %collective-permute-start.3 = (bf16[8,112,256]{2,1,0:T(8,128)(2,1)}, bf16[8,112,256]{2,1,0:T(8,128)(2,1)}, u32[]{:S(2)}, u32[]{:S(2)}) collective-permute-start(bf16[8,112,256]{2,1,0:T(8,128)(2,1)} %slice.33), channel_id=1, source_target_pairs={{0,128},{8,136},{16,144},{24,152},{32,160},{40,168},{48,176},{56,1... | collective-permute-start | bytes 1376264 | tf_op jit(solution)/shard_map/ppermute | solution.py:48
  42.0 0.0 copy-start.10
  42.0 0.0 copy-start.11
  42.0 1.3 %collective-permute-start.4 = (bf16[512,256]{1,0:T(8,128)(2,1)S(1)}, bf16[512,256]{1,0:T(8,128)(2,1)S(1)}, u32[]{:S(2)}, u32[]{:S(2)}) collective-permute-start(bf16[512,256]{1,0:T(8,128)(2,1)S(1)} %slice.30), channel_id=1, source_target_pairs={{0,192},{8,200},{16,208},{24,216},{32,224},{40,232},{48,240},{56,2... | collective-permute-start | bytes 786440 | tf_op jit(solution)/shard_map/ppermute | solution.py:48
  43.3 0.9 shard_map.120.seen
  44.3 0.0 copy-done.10
  44.3 0.0 copy-done.11
  44.3 0.1 pad_maximum_fusion.2.rates
  44.4 14.2 %all-to-all-done.1.received = bf16[8,432,128]{2,1,0:T(8,128)(2,1)S(1)} async-done(((bf16[8,432,128]{2,1,0:T(8,128)(2,1)}), bf16[8,432,128]{2,1,0:T(8,128)(2,1)S(1)}, u32[]{:S(2)}, u32[]{:S(2)}) %all-to-all-start.1) | async-done | bytes 884768 | tf_op jit(solution)/shard_map/all_to_all | solution.py:43
  58.6 1.3 %shard_map.119 = (f32[1024,128]{1,0:T(8,128)S(1)}, f32[16,256]{1,0:T(8,128)S(1)}) custom-call(s32[20]{0:T(128)S(1)} %concatenate.12.info, f32[32]{0:T(128)S(1)} %pad_maximum_fusion.2.rates, bf16[8,432,128]{2,1,0:T(8,128)(2,1)S(1)} %all-to-all-done.1.received), custom_call_target="tpu_custom_call" | custom-call | bytes 2097152 | tf_op jit(solution)/shard_map/pallas_call | solution.py:538
  59.9 1.5 %shard_map.121 = (f32[1024,128]{1,0:T(8,128)S(1)}, f32[1024,128]{1,0:T(8,128)S(1)}, f32[1024,128]{1,0:T(8,128)S(1)}) custom-call(bf16[8,432,128]{2,1,0:T(8,128)(2,1)S(1)} %all-to-all-done.1.received, bf16[1024,256]{1,0:T(8,128)(2,1)S(1)} %bitcast.18, f32[1024,128]{1,0:T(8,128)S(1)} %shard_map.120.seen), custom_call_target="tpu_custom_call" | custom-call | bytes 2097152 | tf_op jit(solution)/shard_map/pallas_call | solution.py:538
  61.4 0.0 collective-permute-done.4.back3
  61.4 0.0 collective-permute-done.3.back2
  61.4 0.0 collective-permute-done.2.back1
  61.5 0.0 copy-start.5
  61.5 0.6 collective-permute-start.5
  62.1 1.4 %shard_map.122.attended = bf16[1040,128]{1,0:T(8,128)(2,1)S(1)} custom-call(s32[20]{0:T(128)S(1)} %concatenate.12.info, bf16[8,432,128]{2,1,0:T(8,128)(2,1)S(1)} %all-to-all-done.1.received, bf16[1024,256]{1,0:T(8,128)(2,1)S(1)} %collective-permute-done.2.back1, bf16[8,112,256]{2,1,0:T(8,128)(2,1)} %collective-permute-done.3.back2, ...), custom_call_target="tpu_custom_call" | custom-call | flops 4294967296 | bytes 2097152 | tf_op jit(solution)/shard_map/pallas_call | solution.py:538
  63.5 0.1 collective-permute-done.5.other
  63.6 0.0 copy-done.5
  63.6 2.1 %shard_map.123 = (bf16[1024,128]{1,0:T(8,128)(2,1)S(1)}, bf16[4,144,256]{2,1,0:T(8,128)(2,1)}) custom-call(s32[20]{0:T(128)S(1)} %concatenate.12.info, bf16[1040,128]{1,0:T(8,128)(2,1)S(1)} %shard_map.122.attended, bf16[8,432,128]{2,1,0:T(8,128)(2,1)S(1)} %all-to-all-done.1.received, bf16[8,256,128]{2,1,0:T(8,128)(2,1)S(1)} %collective-permute-done.5.other, ...), custom_call_target="tpu_custom_call" | custom-call | bytes 2097152 | tf_op jit(solution)/shard_map/pallas_call | solution.py:538
  65.7 0.0 copy-done.2
  65.7 9.0 %all-to-all-start.2 = ((bf16[4,144,256]{2,1,0:T(8,128)(2,1)}), bf16[4,144,256]{2,1,0:T(8,128)(2,1)S(1)}, u32[]{:S(2)}, u32[]{:S(2)}) async-start(bf16[4,144,256]{2,1,0:T(8,128)(2,1)} %get-tuple-element.44), calls=%async_computation.2 | async-start | bytes 589824 | tf_op jit(solution)/shard_map/all_to_all | solution.py:647
  74.7 1.0 %copy-done.3 = bf16[8,256,128]{2,1,0:T(8,128)(2,1)S(1)} copy-done((bf16[8,256,128]{2,1,0:T(8,128)(2,1)S(1)}, bf16[8,256,128]{2,1,0:T(8,128)(2,1)}, u32[]{:S(2)}) %copy-start.3) | copy-done | bytes 524312
  75.7 3.1 %shard_map.124 = (f32[1024,128]{1,0:T(8,128)S(1)}, f32[1024,128]{1,0:T(8,128)S(1)}, bf16[1024,256]{1,0:T(8,128)(2,1)S(1)}) custom-call(s32[20]{0:T(128)S(1)} %concatenate.12.info, f32[32]{0:T(128)S(1)} %pad_maximum_fusion.2.rates, bf16[8,432,128]{2,1,0:T(8,128)(2,1)S(1)} %all-to-all-done.1.received, bf16[8,256,128]{2,1,0:T(8,128)(2,1)S(1)} %copy-done.3, ...), custom_call_target="tpu_custom_call" | custom-call | flops 1073741824 | bytes 2097152 | tf_op jit(solution)/shard_map/pallas_call | solution.py:538
  78.8 2.7 %all-to-all-done.2.handed = bf16[4,144,256]{2,1,0:T(8,128)(2,1)S(1)} async-done(((bf16[4,144,256]{2,1,0:T(8,128)(2,1)}), bf16[4,144,256]{2,1,0:T(8,128)(2,1)S(1)}, u32[]{:S(2)}, u32[]{:S(2)}) %all-to-all-start.2) | async-done | bytes 294944 | tf_op jit(solution)/shard_map/all_to_all | solution.py:647
  81.5 0.9 shard_map.125
  82.4 0.0 copy-start.1
  82.4 13.8 %all_to_all.30.y = bf16[8,128,128]{2,1,0:T(8,128)(2,1)S(1)} all-to-all(bf16[8,128,128]{2,1,0:T(8,128)(2,1)S(1)} %bitcast.19), channel_id=1, replica_groups={{0,8,16,24,32,40,48,56},{64,72,80,88,96,104,112,120},{128,136,144,152,1..., dimensions={0} | all-to-all | bytes 524288 | tf_op jit(solution)/shard_map/all_to_all | solution.py:43
  96.2 0.0 copy-done.1
  96.2 0.3 shard_map.126.sums
  96.5 2.8 %collective-permute-start.6 = (f32[128,128]{1,0:T(8,128)S(1)}, f32[128,128]{1,0:T(8,128)S(1)}, u32[]{:S(2)}, u32[]{:S(2)}) collective-permute-start(f32[128,128]{1,0:T(8,128)S(1)} %shard_map.126.sums), channel_id=1, source_target_pairs={{0,1},{1,0},{2,3},{3,2},{4,5},{5,4},{6,7},{7,6},{8,9},{9,8},{10,11... | collective-permute-start | bytes 196616 | tf_op jit(solution)/shard_map/ppermute | solution.py:57
  99.2 0.9 collective-permute-done.6.partner
  100.1 0.9 shard_map.127
  (15 shorter events, 0.1 us)
Async XLA Ops:
  0.0 16.1 %copy-start = (bf16[128,2,4,256]{3,2,1,0:T(4,128)(2,1)S(1)}, bf16[128,2,4,256]{3,2,1,0:T(4,128)(2,1)}, u32[]{:S(2)}) copy-start(bf16[128,2,4,256]{3,2,1,0:T(4,128)(2,1)} %param.17) | copy-start | bytes 1572868
  0.0 0.8 copy-start.7
  1.7 26.4 %all-to-all-start = ((bf16[8,128,256]{2,1,0:T(8,128)(2,1)}), bf16[8,128,256]{2,1,0:T(8,128)(2,1)S(1)}, u32[]{:S(2)}, u32[]{:S(2)}) async-start(bf16[8,128,256]{2,1,0:T(8,128)(2,1)} %broadcast_select_fusion), calls=%async_computation | async-start | bytes 1048576 | tf_op jit(solution)/shard_map/all_to_all | solution.py:43
  10.7 0.7 slice-start.1
  10.7 0.7 slice-start.2
  11.4 11.3 %collective-permute-start.1 = (bf16[32,128]{1,0:T(8,128)(2,1)S(1)}, bf16[32,128]{1,0:T(8,128)(2,1)S(1)}, u32[]{:S(2)}, u32[]{:S(2)}) collective-permute-start(bf16[32,128]{1,0:T(8,128)(2,1)S(1)} %pad_maximum_fusion.1), channel_id=1, source_target_pairs={{0,128},{8,136},{16,144},{24,152},{32,160},{40,168},{48,176},{56,1... | collective-permute-start | bytes 24584 | tf_op jit(solution)/shard_map/ppermute | solution.py:48
  16.3 0.8 slice-start
  16.3 6.4 %copy-start.4 = (bf16[128,1024]{1,0:T(8,128)(2,1)S(1)}, bf16[128,1024]{1,0:T(8,128)(2,1)}, u32[]{:S(2)}) copy-start(bf16[128,1024]{1,0:T(8,128)(2,1)} %queries.1) | copy-start | bytes 786436
  17.0 5.7 %collective-permute-start = (bf16[16,1280]{1,0:T(8,128)(2,1)S(1)}, bf16[16,1280]{1,0:T(8,128)(2,1)S(1)}, u32[]{:S(2)}, u32[]{:S(2)}) collective-permute-start(bf16[16,1280]{1,0:T(8,128)(2,1)S(1)} %pad_maximum_fusion), channel_id=1, source_target_pairs={{0,8},{8,16},{16,24},{24,32},{32,40},{40,48},{48,56},{56,64},{64,7... | collective-permute-start | bytes 122888 | tf_op jit(solution)/shard_map/ppermute | solution.py:52
  21.1 0.7 copy-start.8
  22.0 0.7 copy-start.9
  28.1 30.4 %all-to-all-start.1 = ((bf16[8,432,128]{2,1,0:T(8,128)(2,1)}), bf16[8,432,128]{2,1,0:T(8,128)(2,1)S(1)}, u32[]{:S(2)}, u32[]{:S(2)}) async-start(bf16[8,432,128]{2,1,0:T(8,128)(2,1)} %shard_map.118), calls=%async_computation.1 | async-start | bytes 1769472 | tf_op jit(solution)/shard_map/all_to_all | solution.py:43
  32.9 28.5 %collective-permute-start.2 = (bf16[1024,256]{1,0:T(8,128)(2,1)S(1)}, bf16[1024,256]{1,0:T(8,128)(2,1)S(1)}, u32[]{:S(2)}, u32[]{:S(2)}) collective-permute-start(bf16[1024,256]{1,0:T(8,128)(2,1)S(1)} %bitcast.16), channel_id=1, source_target_pairs={{0,64},{8,72},{16,80},{24,88},{32,96},{40,104},{48,112},{56,120},{... | collective-permute-start | bytes 1572872 | tf_op jit(solution)/shard_map/ppermute | solution.py:48
  36.8 24.6 %collective-permute-start.3 = (bf16[8,112,256]{2,1,0:T(8,128)(2,1)}, bf16[8,112,256]{2,1,0:T(8,128)(2,1)}, u32[]{:S(2)}, u32[]{:S(2)}) collective-permute-start(bf16[8,112,256]{2,1,0:T(8,128)(2,1)} %slice.33), channel_id=1, source_target_pairs={{0,128},{8,136},{16,144},{24,152},{32,160},{40,168},{48,176},{56,1... | collective-permute-start | bytes 1376264 | tf_op jit(solution)/shard_map/ppermute | solution.py:48
  42.0 2.3 %copy-start.10 = (f32[16]{0:T(128)S(1)}, f32[16]{0:T(128)}, u32[]{:S(2)}) copy-start(f32[16]{0:T(128)} %param.20) | copy-start | bytes 196
  42.0 2.3 %copy-start.11 = (f32[16]{0:T(128)S(1)}, f32[16]{0:T(128)}, u32[]{:S(2)}) copy-start(f32[16]{0:T(128)} %param.19) | copy-start | bytes 196
  42.0 19.4 %collective-permute-start.4 = (bf16[512,256]{1,0:T(8,128)(2,1)S(1)}, bf16[512,256]{1,0:T(8,128)(2,1)S(1)}, u32[]{:S(2)}, u32[]{:S(2)}) collective-permute-start(bf16[512,256]{1,0:T(8,128)(2,1)S(1)} %slice.30), channel_id=1, source_target_pairs={{0,192},{8,200},{16,208},{24,216},{32,224},{40,232},{48,240},{56,2... | collective-permute-start | bytes 786440 | tf_op jit(solution)/shard_map/ppermute | solution.py:48
  61.5 2.1 %copy-start.5 = (f32[4,1024]{1,0:T(4,128)S(1)}, f32[4,1024]{1,0:T(4,128)}, u32[]{:S(2)}) copy-start(f32[4,1024]{1,0:T(4,128)} %taps.1) | copy-start | bytes 49156
  61.5 2.1 %collective-permute-start.5 = (bf16[8,256,128]{2,1,0:T(8,128)(2,1)S(1)}, bf16[8,256,128]{2,1,0:T(8,128)(2,1)S(1)}, u32[]{:S(2)}, u32[]{:S(2)}) collective-permute-start(bf16[8,256,128]{2,1,0:T(8,128)(2,1)S(1)} %slice.31), channel_id=1, source_target_pairs={{0,1},{1,0},{2,3},{3,2},{4,5},{5,4},{6,7},{7,6},{8,9},{9,8},{10,11... | collective-permute-start | bytes 1572872 | tf_op jit(solution)/shard_map/ppermute | solution.py:57
  63.6 2.1 %copy-start.2 = (bf16[8,256,128]{2,1,0:T(8,128)(2,1)}, bf16[8,256,128]{2,1,0:T(8,128)(2,1)S(1)}, u32[]{:S(2)}) copy-start(bf16[8,256,128]{2,1,0:T(8,128)(2,1)S(1)} %collective-permute-done.5.other) | copy-start | bytes 1572868
  65.7 15.8 %all-to-all-start.2 = ((bf16[4,144,256]{2,1,0:T(8,128)(2,1)}), bf16[4,144,256]{2,1,0:T(8,128)(2,1)S(1)}, u32[]{:S(2)}, u32[]{:S(2)}) async-start(bf16[4,144,256]{2,1,0:T(8,128)(2,1)} %get-tuple-element.44), calls=%async_computation.2 | async-start | bytes 589824 | tf_op jit(solution)/shard_map/all_to_all | solution.py:647
  74.7 1.0 %copy-start.3 = (bf16[8,256,128]{2,1,0:T(8,128)(2,1)S(1)}, bf16[8,256,128]{2,1,0:T(8,128)(2,1)}, u32[]{:S(2)}) copy-start(bf16[8,256,128]{2,1,0:T(8,128)(2,1)} %copy-done.2) | copy-start | bytes 1572868
  82.4 13.8 %copy-start.1 = (bf16[128,1024]{1,0:T(8,128)(2,1)S(1)}, bf16[128,1024]{1,0:T(8,128)(2,1)}, u32[]{:S(2)}) copy-start(bf16[128,1024]{1,0:T(8,128)(2,1)} %gate.3) | copy-start | bytes 786436
  96.2 4.0 %copy-start.6 = (f32[1024]{0:T(1024)S(1)}, f32[1024]{0:T(1024)}, u32[]{:S(2)}) copy-start(f32[1024]{0:T(1024)} %param.23) | copy-start | bytes 12292
  96.5 3.7 %collective-permute-start.6 = (f32[128,128]{1,0:T(8,128)S(1)}, f32[128,128]{1,0:T(8,128)S(1)}, u32[]{:S(2)}, u32[]{:S(2)}) collective-permute-start(f32[128,128]{1,0:T(8,128)S(1)} %shard_map.126.sums), channel_id=1, source_target_pairs={{0,1},{1,0},{2,3},{3,2},{4,5},{5,4},{6,7},{7,6},{8,9},{9,8},{10,11... | collective-permute-start | bytes 196616 | tf_op jit(solution)/shard_map/ppermute | solution.py:57

commit v4 on v3

--- a/solution.py
+++ b/solution.py
@@ -261,6 +261,11 @@
         product = jnp.dot(jnp.concatenate(weights[j], 0), values, preferred_element_type=F32)
         rows = slice(j * CHUNK, ROW)
         summed[rows] = product if j == 0 else summed[rows] + product
+
+
+def ahead_kernel(info, rates, received, own, seen, weigh, decays, top, total, summed):
+    weights_kernel(info, rates, received, weigh, decays)
+    attend_own_kernel(received, own, seen, top, total, summed)
 
 
 def attend_kernel(
@@ -631,13 +636,13 @@
     received = exchange_near(packed.reshape(NEAR * PACK_ROWS, HEAD)).reshape(
         NEAR, PACK_ROWS, HEAD
     )
-    weigh, decays = call(
-        weights_kernel,
-        [((ROW, HEAD), F32), ((16, STATE), F32)],
-        (info, rates, received),
+    weigh, decays, *own_part = call(
+        ahead_kernel,
+        [((ROW, HEAD), F32), ((16, STATE), F32)] + [((ROW, HEAD), F32)] * 3,
+        (info, rates, received, own, seen),
         smem=2,
-    )
-    own_part = call(attend_own_kernel, [((ROW, HEAD), F32)] * 3, (received, own, seen), mib=7)
+        mib=7,
+    )
     received, weigh, back1, back2, back3, *own_part = lax.optimization_barrier(
         (received, weigh, back1, back2, back3, *own_part)
     )

time: 101 us -> 99.2 us (0.982); the launches traced: 101 us -> 98.1 us
  starting transfers between devices: 43.7 us -> 42.5 us
  blocking collectives: 13.8 us -> 12.6 us
    all_to_all x1, starting transfers between devices: 8.98 us -> 7.8 us  [on_device(): lax.all_to_all(handed.reshape(FAR * (HEAD + 16), STATE), 'ctx', 0, 0, axi...]
    all_to_all x1, blocking collectives: 13.8 us -> 12.6 us  [exchange_near(): lax.all_to_all(x, 'ctx', 0, 0, axis_index_groups=near_groups(), tiled=True)]
    pallas_call x10 -> x9, Pallas kernels: 14.2 us -> 13.6 us  [call(): pl.pallas_call(kernel, out_shape=shapes[0] if single else shapes, in_spec...]
where the time goes in v4:
time: 99.2 us; the launch traced here: 98.1 us
  starting transfers between devices  42.5 us (43%)
  waiting for transfers between devices  21.6 us (22%)
  Pallas kernels  13.6 us (14%)
  blocking collectives  12.6 us (13%)
  local copies, waits for them, and re-layouts  6.61 us (7%)
    all_to_all x2, waiting for transfers between devices, exchange_near(): lax.all_to_all(x, 'ctx', 0, 0, axis_index_groups=near_groups(), tiled=True)  17.9 us
    ppermute x4, starting transfers between devices, from_row_behind(): return lax.ppermute(x, 'ctx', pairs)  14.2 us
    all_to_all x2, starting transfers between devices, exchange_near(): lax.all_to_all(x, 'ctx', 0, 0, axis_index_groups=near_groups(), tiled=True)  13.8 us
    pallas_call x9, Pallas kernels, call(): pl.pallas_call(kernel, out_shape=shapes[0] if single else shapes, in_spec...  13.6 us
    all_to_all x1, blocking collectives, exchange_near(): lax.all_to_all(x, 'ctx', 0, 0, axis_index_groups=near_groups(), tiled=True)  12.6 us
    all_to_all x1, starting transfers between devices, on_device(): lax.all_to_all(handed.reshape(FAR * (HEAD + 16), STATE), 'ctx', 0, 0, axi...  7.8 us
    ppermute x1, starting transfers between devices, from_shard_behind(): return lax.ppermute(x, 'ctx', [(i, i + 1) for i in range(NEAR * FAR - 1)])  3.36 us
    ppermute x2, starting transfers between devices, with_partner(): return lax.ppermute(x, 'tp', [(t, t ^ 1) for t in range(count)])  3.35 us
  transfers between devices with their start and end apart: 10, of which 5 were waited for; matrix products, arithmetic and copies ran while one was open for 2% of the time, Pallas kernels for 10%

profile of v4, /device:TPU:1, one launch (start us, length us, event | category | flops | bytes accessed | tf_op | source)
XLA Modules:
  0.0 98.1 jit_solution(17971498753656050974)
XLA Ops:
  0.0 0.0 copy-start
  0.0 0.0 copy-start.7
  0.0 0.8 pad.8
  0.9 0.0 copy-done.7
  0.9 0.8 broadcast_select_fusion
  1.7 9.0 %all-to-all-start = ((bf16[8,128,256]{2,1,0:T(8,128)(2,1)}), bf16[8,128,256]{2,1,0:T(8,128)(2,1)S(1)}, u32[]{:S(2)}, u32[]{:S(2)}) async-start(bf16[8,128,256]{2,1,0:T(8,128)(2,1)} %broadcast_select_fusion), calls=%async_computation | async-start | bytes 1048576 | tf_op jit(solution)/shard_map/all_to_all | solution.py:43
  10.7 0.0 slice-start.2
  10.8 0.7 slice-done.1
  11.4 0.0 slice-done.2
  11.4 4.6 %collective-permute-start.1 = (bf16[32,128]{1,0:T(8,128)(2,1)S(1)}, bf16[32,128]{1,0:T(8,128)(2,1)S(1)}, u32[]{:S(2)}, u32[]{:S(2)}) collective-permute-start(bf16[32,128]{1,0:T(8,128)(2,1)S(1)} %pad_maximum_fusion.1), channel_id=1, source_target_pairs={{0,128},{8,136},{16,144},{24,152},{32,160},{40,168},{48,176},{56,1... | collective-permute-start | bytes 24584 | tf_op jit(solution)/shard_map/ppermute | solution.py:48
  16.1 0.0 copy-done
  16.1 0.1 constant_dynamic-slice_fusion.1
  16.3 0.0 slice-start
  16.3 0.0 copy-start.4
  16.3 0.7 slice-done
  17.0 3.4 %collective-permute-start = (bf16[16,1280]{1,0:T(8,128)(2,1)S(1)}, bf16[16,1280]{1,0:T(8,128)(2,1)S(1)}, u32[]{:S(2)}, u32[]{:S(2)}) collective-permute-start(bf16[16,1280]{1,0:T(8,128)(2,1)S(1)} %pad_maximum_fusion), channel_id=1, source_target_pairs={{0,8},{8,16},{16,24},{24,32},{32,40},{40,48},{48,56},{56,64},{64,7... | collective-permute-start | bytes 122888 | tf_op jit(solution)/shard_map/ppermute | solution.py:52
  20.4 0.7 constant_dynamic-slice_fusion
  21.2 0.0 copy-start.8
  21.2 0.7 copy-done.8
  21.9 0.1 copy.16.steps
  22.0 0.0 copy-start.9
  22.0 0.6 copy-done.9
  22.6 0.1 concatenate.12.info
  22.7 0.0 collective-permute-done.1.side
  22.7 0.0 collective-permute-done.rim
  22.7 0.0 copy-done.4
  22.7 1.8 %shard_map.118 = bf16[8,432,128]{2,1,0:T(8,128)(2,1)} custom-call(s32[20]{0:T(128)S(1)} %concatenate.12.info, bf16[128,1024]{1,0:T(8,128)(2,1)S(1)} %copy-done.4, f32[128,16]{1,0:T(8,128)S(1)} %copy.16.steps, bf16[128,256]{1,0:T(8,128)(2,1)S(1)} %bitcast.20, bf16[16,1280]{1,0:T(8,128)(2,1)S(1)} %collective-permute-done.rim, f32[4,256]{1,0:T(4,128)S(1)} %bitcast.21, ...), custom_call_target="tpu_custom_call" | custom-call | bytes 2097152 | tf_op jit(solution)/shard_map/pallas_call | solution.py:543
  24.5 3.7 %all-to-all-done = bf16[8,128,256]{2,1,0:T(8,128)(2,1)S(1)} async-done(((bf16[8,128,256]{2,1,0:T(8,128)(2,1)}), bf16[8,128,256]{2,1,0:T(8,128)(2,1)S(1)}, u32[]{:S(2)}, u32[]{:S(2)}) %all-to-all-start) | async-done | bytes 524320 | tf_op jit(solution)/shard_map/all_to_all | solution.py:43
  28.1 4.8 %all-to-all-start.1 = ((bf16[8,432,128]{2,1,0:T(8,128)(2,1)}), bf16[8,432,128]{2,1,0:T(8,128)(2,1)S(1)}, u32[]{:S(2)}, u32[]{:S(2)}) async-start(bf16[8,432,128]{2,1,0:T(8,128)(2,1)} %shard_map.118), calls=%async_computation.1 | async-start | bytes 1769472 | tf_op jit(solution)/shard_map/all_to_all | solution.py:43
  32.9 3.1 %collective-permute-start.2 = (bf16[1024,256]{1,0:T(8,128)(2,1)S(1)}, bf16[1024,256]{1,0:T(8,128)(2,1)S(1)}, u32[]{:S(2)}, u32[]{:S(2)}) collective-permute-start(bf16[1024,256]{1,0:T(8,128)(2,1)S(1)} %bitcast.16), channel_id=1, source_target_pairs={{0,64},{8,72},{16,80},{24,88},{32,96},{40,104},{48,112},{56,120},{... | collective-permute-start | bytes 1572872 | tf_op jit(solution)/shard_map/ppermute | solution.py:48
  36.0 0.8 slice.33
  36.9 5.1 %collective-permute-start.3 = (bf16[8,112,256]{2,1,0:T(8,128)(2,1)}, bf16[8,112,256]{2,1,0:T(8,128)(2,1)}, u32[]{:S(2)}, u32[]{:S(2)}) collective-permute-start(bf16[8,112,256]{2,1,0:T(8,128)(2,1)} %slice.33), channel_id=1, source_target_pairs={{0,128},{8,136},{16,144},{24,152},{32,160},{40,168},{48,176},{56,1... | collective-permute-start | bytes 1376264 | tf_op jit(solution)/shard_map/ppermute | solution.py:48
  42.0 0.0 copy-start.10
  42.0 0.0 copy-start.11
  42.0 1.3 %collective-permute-start.4 = (bf16[512,256]{1,0:T(8,128)(2,1)S(1)}, bf16[512,256]{1,0:T(8,128)(2,1)S(1)}, u32[]{:S(2)}, u32[]{:S(2)}) collective-permute-start(bf16[512,256]{1,0:T(8,128)(2,1)S(1)} %slice.30), channel_id=1, source_target_pairs={{0,192},{8,200},{16,208},{24,216},{32,224},{40,232},{48,240},{56,2... | collective-permute-start | bytes 786440 | tf_op jit(solution)/shard_map/ppermute | solution.py:48
  43.3 0.9 shard_map.119.seen
  44.3 0.0 copy-done.10
  44.3 0.0 copy-done.11
  44.3 0.1 pad_maximum_fusion.2.rates
  44.4 14.2 %all-to-all-done.1.received = bf16[8,432,128]{2,1,0:T(8,128)(2,1)S(1)} async-done(((bf16[8,432,128]{2,1,0:T(8,128)(2,1)}), bf16[8,432,128]{2,1,0:T(8,128)(2,1)S(1)}, u32[]{:S(2)}, u32[]{:S(2)}) %all-to-all-start.1) | async-done | bytes 884768 | tf_op jit(solution)/shard_map/all_to_all | solution.py:43
  58.6 2.2 %shard_map.120 = (f32[1024,128]{1,0:T(8,128)S(1)}, f32[16,256]{1,0:T(8,128)S(1)}, f32[1024,128]{1,0:T(8,128)S(1)}, f32[1024,128]{1,0:T(8,128)S(1)}, f32[1024,128]{1,0:T(8,128)S(1)}) custom-call(s32[20]{0:T(128)S(1)} %concatenate.12.info, f32[32]{0:T(128)S(1)} %pad_maximum_fusion.2.rates, bf16[8,432,128]{2,1,0:T(8,128)(2,1)S(1)} %all-to-all-done.1.received, ...), custom_call_target="tpu_custom_call" | custom-call | bytes 2097152 | tf_op jit(solution)/shard_map/pallas_call | solution.py:543
  60.8 0.0 collective-permute-done.4.back3
  60.8 0.0 collective-permute-done.3.back2
  60.8 0.0 collective-permute-done.2.back1
  60.9 0.0 copy-start.5
  60.9 0.6 collective-permute-start.5
  61.5 1.4 %shard_map.121.attended = bf16[1040,128]{1,0:T(8,128)(2,1)S(1)} custom-call(s32[20]{0:T(128)S(1)} %concatenate.12.info, bf16[8,432,128]{2,1,0:T(8,128)(2,1)S(1)} %all-to-all-done.1.received, bf16[1024,256]{1,0:T(8,128)(2,1)S(1)} %collective-permute-done.2.back1, bf16[8,112,256]{2,1,0:T(8,128)(2,1)} %collective-permute-done.3.back2, ...), custom_call_target="tpu_custom_call" | custom-call | flops 4294967296 | bytes 2097152 | tf_op jit(solution)/shard_map/pallas_call | solution.py:543
  62.9 0.1 collective-permute-done.5.other
  63.0 0.0 copy-done.5
  63.0 2.1 %shard_map.122 = (bf16[1024,128]{1,0:T(8,128)(2,1)S(1)}, bf16[4,144,256]{2,1,0:T(8,128)(2,1)}) custom-call(s32[20]{0:T(128)S(1)} %concatenate.12.info, bf16[1040,128]{1,0:T(8,128)(2,1)S(1)} %shard_map.121.attended, bf16[8,432,128]{2,1,0:T(8,128)(2,1)S(1)} %all-to-all-done.1.received, bf16[8,256,128]{2,1,0:T(8,128)(2,1)S(1)} %collective-permute-done.5.other, ...), custom_call_target="tpu_custom_call" | custom-call | bytes 2097152 | tf_op jit(solution)/shard_map/pallas_call | solution.py:543
  65.1 0.0 copy-done.2
  65.1 7.8 %all-to-all-start.2 = ((bf16[4,144,256]{2,1,0:T(8,128)(2,1)}), bf16[4,144,256]{2,1,0:T(8,128)(2,1)S(1)}, u32[]{:S(2)}, u32[]{:S(2)}) async-start(bf16[4,144,256]{2,1,0:T(8,128)(2,1)} %get-tuple-element.44), calls=%async_computation.2 | async-start | bytes 589824 | tf_op jit(solution)/shard_map/all_to_all | solution.py:652
  72.9 1.0 %copy-done.3 = bf16[8,256,128]{2,1,0:T(8,128)(2,1)S(1)} copy-done((bf16[8,256,128]{2,1,0:T(8,128)(2,1)S(1)}, bf16[8,256,128]{2,1,0:T(8,128)(2,1)}, u32[]{:S(2)}) %copy-start.3) | copy-done | bytes 524312
  73.9 3.1 %shard_map.123 = (f32[1024,128]{1,0:T(8,128)S(1)}, f32[1024,128]{1,0:T(8,128)S(1)}, bf16[1024,256]{1,0:T(8,128)(2,1)S(1)}) custom-call(s32[20]{0:T(128)S(1)} %concatenate.12.info, f32[32]{0:T(128)S(1)} %pad_maximum_fusion.2.rates, bf16[8,432,128]{2,1,0:T(8,128)(2,1)S(1)} %all-to-all-done.1.received, bf16[8,256,128]{2,1,0:T(8,128)(2,1)S(1)} %copy-done.3, ...), custom_call_target="tpu_custom_call" | custom-call | flops 1073741824 | bytes 2097152 | tf_op jit(solution)/shard_map/pallas_call | solution.py:543
  77.0 2.7 %all-to-all-done.2.handed = bf16[4,144,256]{2,1,0:T(8,128)(2,1)S(1)} async-done(((bf16[4,144,256]{2,1,0:T(8,128)(2,1)}), bf16[4,144,256]{2,1,0:T(8,128)(2,1)S(1)}, u32[]{:S(2)}, u32[]{:S(2)}) %all-to-all-start.2) | async-done | bytes 294944 | tf_op jit(solution)/shard_map/all_to_all | solution.py:652
  79.7 0.9 shard_map.124
  80.6 0.0 copy-start.1
  80.6 12.6 %all_to_all.30.y = bf16[8,128,128]{2,1,0:T(8,128)(2,1)S(1)} all-to-all(bf16[8,128,128]{2,1,0:T(8,128)(2,1)S(1)} %bitcast.19), channel_id=1, replica_groups={{0,8,16,24,32,40,48,56},{64,72,80,88,96,104,112,120},{128,136,144,152,1..., dimensions={0} | all-to-all | bytes 524288 | tf_op jit(solution)/shard_map/all_to_all | solution.py:43
  93.2 0.0 copy-done.1
  93.2 0.3 shard_map.125.sums
  93.5 2.8 %collective-permute-start.6 = (f32[128,128]{1,0:T(8,128)S(1)}, f32[128,128]{1,0:T(8,128)S(1)}, u32[]{:S(2)}, u32[]{:S(2)}) collective-permute-start(f32[128,128]{1,0:T(8,128)S(1)} %shard_map.125.sums), channel_id=1, source_target_pairs={{0,1},{1,0},{2,3},{3,2},{4,5},{5,4},{6,7},{7,6},{8,9},{9,8},{10,11... | collective-permute-start | bytes 196616 | tf_op jit(solution)/shard_map/ppermute | solution.py:57
  96.3 0.9 collective-permute-done.6.partner
  97.2 0.0 copy-done.6
  97.2 0.9 shard_map.126
  (14 shorter events, 0.1 us)
Async XLA Ops:
  0.0 16.1 %copy-start = (bf16[128,2,4,256]{3,2,1,0:T(4,128)(2,1)S(1)}, bf16[128,2,4,256]{3,2,1,0:T(4,128)(2,1)}, u32[]{:S(2)}) copy-start(bf16[128,2,4,256]{3,2,1,0:T(4,128)(2,1)} %param.17) | copy-start | bytes 1572868
  0.0 0.8 copy-start.7
  1.7 26.4 %all-to-all-start = ((bf16[8,128,256]{2,1,0:T(8,128)(2,1)}), bf16[8,128,256]{2,1,0:T(8,128)(2,1)S(1)}, u32[]{:S(2)}, u32[]{:S(2)}) async-start(bf16[8,128,256]{2,1,0:T(8,128)(2,1)} %broadcast_select_fusion), calls=%async_computation | async-start | bytes 1048576 | tf_op jit(solution)/shard_map/all_to_all | solution.py:43
  10.7 0.7 slice-start.1
  10.7 0.7 slice-start.2
  11.4 11.3 %collective-permute-start.1 = (bf16[32,128]{1,0:T(8,128)(2,1)S(1)}, bf16[32,128]{1,0:T(8,128)(2,1)S(1)}, u32[]{:S(2)}, u32[]{:S(2)}) collective-permute-start(bf16[32,128]{1,0:T(8,128)(2,1)S(1)} %pad_maximum_fusion.1), channel_id=1, source_target_pairs={{0,128},{8,136},{16,144},{24,152},{32,160},{40,168},{48,176},{56,1... | collective-permute-start | bytes 24584 | tf_op jit(solution)/shard_map/ppermute | solution.py:48
  16.3 0.8 slice-start
  16.3 6.4 %copy-start.4 = (bf16[128,1024]{1,0:T(8,128)(2,1)S(1)}, bf16[128,1024]{1,0:T(8,128)(2,1)}, u32[]{:S(2)}) copy-start(bf16[128,1024]{1,0:T(8,128)(2,1)} %queries.1) | copy-start | bytes 786436
  17.0 5.7 %collective-permute-start = (bf16[16,1280]{1,0:T(8,128)(2,1)S(1)}, bf16[16,1280]{1,0:T(8,128)(2,1)S(1)}, u32[]{:S(2)}, u32[]{:S(2)}) collective-permute-start(bf16[16,1280]{1,0:T(8,128)(2,1)S(1)} %pad_maximum_fusion), channel_id=1, source_target_pairs={{0,8},{8,16},{16,24},{24,32},{32,40},{40,48},{48,56},{56,64},{64,7... | collective-permute-start | bytes 122888 | tf_op jit(solution)/shard_map/ppermute | solution.py:52
  21.2 0.7 copy-start.8
  22.0 0.7 copy-start.9
  28.1 30.4 %all-to-all-start.1 = ((bf16[8,432,128]{2,1,0:T(8,128)(2,1)}), bf16[8,432,128]{2,1,0:T(8,128)(2,1)S(1)}, u32[]{:S(2)}, u32[]{:S(2)}) async-start(bf16[8,432,128]{2,1,0:T(8,128)(2,1)} %shard_map.118), calls=%async_computation.1 | async-start | bytes 1769472 | tf_op jit(solution)/shard_map/all_to_all | solution.py:43
  32.9 27.9 %collective-permute-start.2 = (bf16[1024,256]{1,0:T(8,128)(2,1)S(1)}, bf16[1024,256]{1,0:T(8,128)(2,1)S(1)}, u32[]{:S(2)}, u32[]{:S(2)}) collective-permute-start(bf16[1024,256]{1,0:T(8,128)(2,1)S(1)} %bitcast.16), channel_id=1, source_target_pairs={{0,64},{8,72},{16,80},{24,88},{32,96},{40,104},{48,112},{56,120},{... | collective-permute-start | bytes 1572872 | tf_op jit(solution)/shard_map/ppermute | solution.py:48
  36.9 23.9 %collective-permute-start.3 = (bf16[8,112,256]{2,1,0:T(8,128)(2,1)}, bf16[8,112,256]{2,1,0:T(8,128)(2,1)}, u32[]{:S(2)}, u32[]{:S(2)}) collective-permute-start(bf16[8,112,256]{2,1,0:T(8,128)(2,1)} %slice.33), channel_id=1, source_target_pairs={{0,128},{8,136},{16,144},{24,152},{32,160},{40,168},{48,176},{56,1... | collective-permute-start | bytes 1376264 | tf_op jit(solution)/shard_map/ppermute | solution.py:48
  42.0 2.3 %copy-start.10 = (f32[16]{0:T(128)S(1)}, f32[16]{0:T(128)}, u32[]{:S(2)}) copy-start(f32[16]{0:T(128)} %param.20) | copy-start | bytes 196
  42.0 2.3 %copy-start.11 = (f32[16]{0:T(128)S(1)}, f32[16]{0:T(128)}, u32[]{:S(2)}) copy-start(f32[16]{0:T(128)} %param.19) | copy-start | bytes 196
  42.0 18.8 %collective-permute-start.4 = (bf16[512,256]{1,0:T(8,128)(2,1)S(1)}, bf16[512,256]{1,0:T(8,128)(2,1)S(1)}, u32[]{:S(2)}, u32[]{:S(2)}) collective-permute-start(bf16[512,256]{1,0:T(8,128)(2,1)S(1)} %slice.30), channel_id=1, source_target_pairs={{0,192},{8,200},{16,208},{24,216},{32,224},{40,232},{48,240},{56,2... | collective-permute-start | bytes 786440 | tf_op jit(solution)/shard_map/ppermute | solution.py:48
  60.9 2.1 %copy-start.5 = (f32[4,1024]{1,0:T(4,128)S(1)}, f32[4,1024]{1,0:T(4,128)}, u32[]{:S(2)}) copy-start(f32[4,1024]{1,0:T(4,128)} %taps.1) | copy-start | bytes 49156
  60.9 2.1 %collective-permute-start.5 = (bf16[8,256,128]{2,1,0:T(8,128)(2,1)S(1)}, bf16[8,256,128]{2,1,0:T(8,128)(2,1)S(1)}, u32[]{:S(2)}, u32[]{:S(2)}) collective-permute-start(bf16[8,256,128]{2,1,0:T(8,128)(2,1)S(1)} %slice.31), channel_id=1, source_target_pairs={{0,1},{1,0},{2,3},{3,2},{4,5},{5,4},{6,7},{7,6},{8,9},{9,8},{10,11... | collective-permute-start | bytes 1572872 | tf_op jit(solution)/shard_map/ppermute | solution.py:57
  63.0 2.1 %copy-start.2 = (bf16[8,256,128]{2,1,0:T(8,128)(2,1)}, bf16[8,256,128]{2,1,0:T(8,128)(2,1)S(1)}, u32[]{:S(2)}) copy-start(bf16[8,256,128]{2,1,0:T(8,128)(2,1)S(1)} %collective-permute-done.5.other) | copy-start | bytes 1572868
  65.1 14.7 %all-to-all-start.2 = ((bf16[4,144,256]{2,1,0:T(8,128)(2,1)}), bf16[4,144,256]{2,1,0:T(8,128)(2,1)S(1)}, u32[]{:S(2)}, u32[]{:S(2)}) async-start(bf16[4,144,256]{2,1,0:T(8,128)(2,1)} %get-tuple-element.44), calls=%async_computation.2 | async-start | bytes 589824 | tf_op jit(solution)/shard_map/all_to_all | solution.py:652
  72.9 1.0 %copy-start.3 = (bf16[8,256,128]{2,1,0:T(8,128)(2,1)S(1)}, bf16[8,256,128]{2,1,0:T(8,128)(2,1)}, u32[]{:S(2)}) copy-start(bf16[8,256,128]{2,1,0:T(8,128)(2,1)} %copy-done.2) | copy-start | bytes 1572868
  80.6 12.6 %copy-start.1 = (bf16[128,1024]{1,0:T(8,128)(2,1)S(1)}, bf16[128,1024]{1,0:T(8,128)(2,1)}, u32[]{:S(2)}) copy-start(bf16[128,1024]{1,0:T(8,128)(2,1)} %gate.3) | copy-start | bytes 786436
  93.2 4.0 %copy-start.6 = (f32[1024]{0:T(1024)S(1)}, f32[1024]{0:T(1024)}, u32[]{:S(2)}) copy-start(f32[1024]{0:T(1024)} %param.23) | copy-start | bytes 12292
  93.5 3.7 %collective-permute-start.6 = (f32[128,128]{1,0:T(8,128)S(1)}, f32[128,128]{1,0:T(8,128)S(1)}, u32[]{:S(2)}, u32[]{:S(2)}) collective-permute-start(f32[128,128]{1,0:T(8,128)S(1)} %shard_map.125.sums), channel_id=1, source_target_pairs={{0,1},{1,0},{2,3},{3,2},{4,5},{5,4},{6,7},{7,6},{8,9},{9,8},{10,11... | collective-permute-start | bytes 196616 | tf_op jit(solution)/shard_map/ppermute | solution.py:57
